TPU v7x, 512 devices: a whole 4x4x16 slice. The times are simulated.
512 devices in a mesh: aa: 32 (over z, x_hi), ba: 16 (over x_lo, y, core).
Axes of the slice: x: 4 (x_hi: 2, x_lo: 2; x = x_hi * 2 + x_lo), y: 4, z: 16, core: 2. Of those that a mesh axis runs over, the one named last changes fastest.
Arguments:
- features_a: bfloat16 [64, 32, 256], P('aa', 'ba'), may hold values from -9 to 9
- features_b: bfloat16 [64, 128, 256], P('ba', 'aa'), may hold values from -9 to 9
- conv_in: float32 [8, 3, 3, 3, 3], replicated, may hold values from -0.625 to 0.625
- bias_in: float32 [8], replicated, may hold values from -1 to 1
- conv_out: float32 [8, 3, 3, 3, 3], replicated, may hold values from -0.25 to 0.25
Outputs:
- log_mutual: float32 [64, 32, 64, 128], P('aa', None, 'ba')
- warped: float32 [64, 32, 256], P('aa', 'ba')
All inputs are finite; a program needn't handle non-finite values.
Results may differ from a plain program's by a relative error of at most 0.0035.
Values may be sent and summed in bfloat16 or wider, within the bound.
A program may use at most 64 MiB of HBM per device.

v0:
```python
import math

import jax
import jax.numpy as jnp
from jax import lax
from jax.sharding import PartitionSpec as P


def padded_2(cells, sides, width):
    for axis, dim in sides:
        count = lax.axis_size(axis)
        ends = count - 1
        head = lax.slice_in_dim(cells, 0, width, axis=dim)
        tail = lax.slice_in_dim(cells, cells.shape[dim] - width, cells.shape[dim], axis=dim)
        cells = jnp.concatenate(
            [
                lax.ppermute(tail, axis, [(i, (i + 1) % count) for i in range(ends)]),
                cells,
                lax.ppermute(head, axis, [((i + 1) % count, i) for i in range(ends)]),
            ],
            axis=dim,
        )
    return cells


def tap_offsets():
    return [
        (step_one, step_two, step_three, step_four)
        for step_one in range(3)
        for step_two in range(3)
        for step_three in range(3)
        for step_four in range(3)
    ]


def spread_taps(padded, kernel, bias_in):
    extent = [size_here - 2 for size_here in padded.shape]
    result = jnp.zeros([kernel.shape[0]] + extent, jnp.float32)
    for offsets in tap_offsets():
        window = padded[
            offsets[0] : offsets[0] + extent[0],
            offsets[1] : offsets[1] + extent[1],
            offsets[2] : offsets[2] + extent[2],
            offsets[3] : offsets[3] + extent[3],
        ]
        result = (
            result
            + kernel[:, offsets[0], offsets[1], offsets[2], offsets[3]].reshape(-1, 1, 1, 1, 1)
            * window[None]
        )
    return jax.nn.relu(result + bias_in.reshape(-1, 1, 1, 1, 1))


def reduce_taps(padded, kernel):
    extent = [size_here - 2 for size_here in padded.shape[1:]]
    result = jnp.zeros(extent, jnp.float32)
    for offsets in tap_offsets():
        window = padded[
            :,
            offsets[0] : offsets[0] + extent[0],
            offsets[1] : offsets[1] + extent[1],
            offsets[2] : offsets[2] + extent[2],
            offsets[3] : offsets[3] + extent[3],
        ]
        result = result + jnp.sum(
            kernel[:, offsets[0], offsets[1], offsets[2], offsets[3]].reshape(-1, 1, 1, 1, 1)
            * window,
            axis=0,
        )
    return result


def dual_norms(values):
    top_a = lax.pmax(jnp.max(values, axis=(0, 1)), "aa")
    top_b = lax.pmax(jnp.max(values, axis=(2, 3)), "ba")
    mass_a = lax.psum(jnp.sum(jnp.exp(values - top_a), axis=(0, 1)), "aa")
    mass_b = lax.psum(jnp.sum(jnp.exp(values - top_b[:, :, None, None]), axis=(2, 3)), "ba")
    norm_a = top_a + jnp.log(mass_a)
    norm_b = top_b + jnp.log(mass_b)
    return (norm_a, norm_b[:, :, None, None])


def local(features_a, features_b, conv_in, bias_in, conv_out):
    channels = features_a.shape[2]
    rows_a = lax.all_gather(features_a, "ba", axis=1, tiled=True)
    rows_b = lax.all_gather(features_b, "aa", axis=1, tiled=True)
    height_a = rows_a.shape[0]
    width_a = rows_a.shape[1]
    height_b = rows_b.shape[0]
    width_b = rows_b.shape[1]
    grid_a = height_a * lax.axis_size("aa")
    grid_b = height_b * lax.axis_size("ba")
    offset = math.log(grid_a * width_a * grid_b * width_b)
    scores = jnp.einsum(
        "xyc,uvc->xyuv", rows_a, rows_b, preferred_element_type=jnp.float32
    ) / math.sqrt(channels)
    norm_a, norm_b = dual_norms(scores)
    matched = jax.nn.softplus(2.0 * scores - norm_a - norm_b + offset)
    rim = padded_2(matched, (("aa", 0), ("ba", 2)), 1)
    hidden = spread_taps(jnp.pad(rim, ((0, 0), (1, 1), (0, 0), (1, 1))), conv_in, bias_in)
    rim_hidden = padded_2(hidden, (("aa", 1), ("ba", 3)), 1)
    filtered = reduce_taps(jnp.pad(rim_hidden, ((0, 0), (0, 0), (1, 1), (0, 0), (1, 1))), conv_out)
    refined = scores + jax.nn.relu(filtered)
    norm_a2, norm_b2 = dual_norms(refined)
    log_mutual = 2.0 * refined - norm_a2 - norm_b2 + offset
    weights = jnp.exp(refined - norm_b2).astype(jnp.bfloat16)
    transfer_terms = jnp.einsum(
        "xyuv,uvc->xyc", weights, rows_b, preferred_element_type=jnp.float32
    )
    warped = lax.psum_scatter(transfer_terms, "ba", scatter_dimension=1, tiled=True)
    return (log_mutual, warped)


def solution(mesh):
    placed = (P("aa", "ba", None), P("ba", "aa", None), P(), P(), P())
    return jax.shard_map(
        local,
        mesh=mesh,
        in_specs=placed,
        out_specs=(P("aa", None, "ba", None), P("aa", "ba", None)),
        check_vma=False,
    )
```

profile of v0, /device:TPU:1, one launch (start us, length us, event | category | flops | bytes accessed | tf_op | source)
XLA Modules:
  0.0 739.9 jit_solution(15070488964184994096)
XLA Ops:
  7.9 70.3 %all_gather.7 = bf16[4,128,256]{2,0,1:T(4,128)(2,1)S(1)} all-gather(bf16[4,4,256]{2,0,1:T(4,128)(2,1)S(1)} %copy.177), channel_id=1, replica_groups=mesh['aa'=32,'ba'=16] {'aa'}, dimensions={1}, use_global_device_ids=true | all-gather | bytes 270336 | tf_op jit(solution)/shard_map/all_gather | solution.py:86
  78.9 33.7 %all_gather.6 = bf16[2,32,256]{2,0,1:T(2,128)(2,1)S(1)} all-gather(bf16[2,2,256]{2,0,1:T(2,128)(2,1)S(1)} %copy.176), channel_id=1, replica_groups=mesh['aa'=32,'ba'=16] {'ba'}, dimensions={1}, use_global_device_ids=true | all-gather | bytes 34816 | tf_op jit(solution)/shard_map/all_gather | solution.py:85
  112.9 58.1 %pmax.28 = f32[4,128]{1,0:T(4,128)S(1)} all-reduce(f32[4,128]{1,0:T(4,128)S(1)} %get-tuple-element.350), channel_id=1, replica_groups=mesh['aa'=32,'ba'=16] {'aa'}, use_global_device_ids=true, to_apply=%region_1.0 | all-reduce | flops 512 | bytes 4096 | tf_op jit(solution)/shard_map/pmax | solution.py:74
  171.2 40.8 %pmax.29 = f32[2,32]{1,0:T(2,128)S(1)} all-reduce(f32[2,32]{1,0:T(2,128)S(1)} %get-tuple-element.94), channel_id=1, replica_groups=mesh['aa'=32,'ba'=16] {'ba'}, use_global_device_ids=true, to_apply=%region_5.0 | all-reduce | flops 64 | bytes 512 | tf_op jit(solution)/shard_map/pmax | solution.py:75
  212.2 27.1 %psum.29 = f32[2,32]{1,0:T(2,128)S(1)} all-reduce(f32[2,32]{1,0:T(2,128)S(1)} %exponential_reduce_fusion.2), channel_id=1, replica_groups=mesh['aa'=32,'ba'=16] {'ba'}, use_global_device_ids=true, to_apply=%region_7.0 | all-reduce | flops 64 | bytes 512 | tf_op jit(solution)/shard_map/psum | solution.py:77
  239.3 61.4 %psum.28 = f32[4,128]{1,0:T(4,128)S(1)} all-reduce(f32[4,128]{1,0:T(4,128)S(1)} %get-tuple-element.93), channel_id=1, replica_groups=mesh['aa'=32,'ba'=16] {'aa'}, use_global_device_ids=true, to_apply=%region_3.0 | all-reduce | flops 512 | bytes 4096 | tf_op jit(solution)/shard_map/psum | solution.py:76
  300.9 1.8 collective-permute-start
  302.7 1.3 collective-permute-start.1
  304.0 1.5 slice_bitcast_fusion.160
  305.5 1.5 slice_bitcast_fusion.159
  307.1 1.5 slice_bitcast_fusion.158
  308.6 1.5 slice_bitcast_fusion.157
  310.1 1.3 slice_bitcast_fusion.156
  311.5 14.0 %collective-permute-start.2 = (f32[4,32,1,128]{3,1,2,0:T(8,128)S(1)}, f32[4,32,1,128]{3,1,2,0:T(8,128)S(1)}, u32[]{:S(2)}, u32[]{:S(2)}) collective-permute-start(f32[4,32,1,128]{3,1,2,0:T(8,128)S(1)} %get-tuple-element.182), channel_id=1, source_target_pairs={{0,1},{1,2},{2,3},{3,4},{4,5},{5,6},{6,7},{7,8},{8,9},{9,10},{10,1... | collective-permute-start | bytes 196616 | tf_op jit(solution)/shard_map/ppermute | solution.py:17
  325.5 4.0 collective-permute-start.3
  329.8 1.3 collective-permute-done.3
  337.1 0.7 copy.207
  340.0 0.8 copy.211
  342.2 0.7 copy.214
  345.2 0.7 copy.219
  348.1 0.7 copy.225
  351.8 0.7 copy.230
  355.4 0.7 copy.235
  359.9 0.7 copy.241
  365.7 0.7 copy.252
  369.4 0.7 copy.257
  371.6 0.8 copy.183
  377.5 0.7 copy.192
  381.9 0.7 copy.260
  382.7 12.3 %add_maximum_fusion = f32[8,2,32,4,128]{4,0,3,2,1:T(8,128)S(1)} fusion(f32[8]{0:T(128)} %param.8, f32[2,32,4,128]{3,2,1,0:T(4,128)} %copy.260, f32[8]{0:T(128)} %get-tuple-element.348, f32[2,32,4,128]{3,2,1,0:T(4,128)} %copy.259, f32[8]{0:T(128)} %get-tuple-element.349, f32[2,32,4,128]{3,2,1,0:T(4,128)} %copy.258, f32[8]{0:T(128)S(1)} %get-tuple-element.270, ...), kind=kLoop, calls=%fused_computation.181 | loop fusion | flops 42729472 | bytes 11668032 | tf_op jit(solution)/shard_map/jit(relu)/max | solution.py:51
  395.1 5.8 collective-permute-start.4
  400.9 1.3 collective-permute-start.5
  402.2 1.5 slice_bitcast_fusion.62
  403.7 1.5 slice_bitcast_fusion.60
  405.2 1.5 slice_bitcast_fusion.59
  406.7 16.9 %collective-permute-done.4 = f32[8,1,32,4,128]{4,0,3,2,1:T(8,128)S(1)} collective-permute-done((f32[8,1,32,4,128]{4,0,3,2,1:T(8,128)S(1)}, f32[8,1,32,4,128]{4,0,3,2,1:T(8,128)S(1)}, u32[]{:S(2)}, u32[]{:S(2)}) %collective-permute-start.4) | collective-permute-done | bytes 524320 | tf_op jit(solution)/shard_map/ppermute | solution.py:17
  423.6 1.1 pad_maximum_fusion.5
  424.7 1.9 collective-permute-start.6
  426.6 2.4 collective-permute-start.7
  429.1 1.4 slice_bitcast_fusion.78
  430.4 1.3 dynamic-slice
  432.3 1.5 slice_bitcast_fusion.61
  433.8 2.5 fusion.71
  436.3 1.1 collective-permute-done.7
  437.8 2.5 fusion.74
  440.2 1.7 fusion.67
  441.9 3.9 select_maximum_fusion
  445.9 3.2 fusion.81
  449.3 3.2 fusion.80
  452.7 3.3 fusion.79
  456.1 3.4 fusion.78
  459.7 3.2 fusion.83
  463.1 4.1 fusion.82
  467.3 4.1 fusion.84
  471.5 4.3 fusion.77
  475.7 3.1 fusion.97
  478.9 61.9 %pmax.30 = f32[4,128]{1,0:T(4,128)S(1)} all-reduce(f32[4,128]{1,0:T(4,128)S(1)} %get-tuple-element.91), channel_id=1, replica_groups=mesh['aa'=32,'ba'=16] {'aa'}, use_global_device_ids=true, to_apply=%region_90.91 | all-reduce | flops 512 | bytes 4096 | tf_op jit(solution)/shard_map/pmax | solution.py:74
  540.8 38.8 %pmax.31 = f32[2,32]{1,0:T(2,128)S(1)} all-reduce(f32[2,32]{1,0:T(2,128)S(1)} %get-tuple-element.92), channel_id=1, replica_groups=mesh['aa'=32,'ba'=16] {'ba'}, use_global_device_ids=true, to_apply=%region_94.95 | all-reduce | flops 64 | bytes 512 | tf_op jit(solution)/shard_map/pmax | solution.py:75
  579.8 27.1 %psum.31 = f32[2,32]{1,0:T(2,128)S(1)} all-reduce(f32[2,32]{1,0:T(2,128)S(1)} %get-tuple-element.90), channel_id=1, replica_groups=mesh['aa'=32,'ba'=16] {'ba'}, use_global_device_ids=true, to_apply=%region_96.97 | all-reduce | flops 64 | bytes 512 | tf_op jit(solution)/shard_map/psum | solution.py:77
  606.9 0.8 convolution_bitcast_fusion
  607.8 62.2 %psum.30 = f32[4,128]{1,0:T(4,128)S(1)} all-reduce(f32[4,128]{1,0:T(4,128)S(1)} %get-tuple-element.89), channel_id=1, replica_groups=mesh['aa'=32,'ba'=16] {'aa'}, use_global_device_ids=true, to_apply=%region_92.93 | all-reduce | flops 512 | bytes 4096 | tf_op jit(solution)/shard_map/psum | solution.py:76
  670.1 0.7 copy.343
  670.8 60.5 %all-reduce.5.cloned.1.call-done = f32[2,32,256]{2,1,0:T(8,128)} async-done(((f32[2,32,256]{2,1,0:T(8,128)}), f32[2,32,256]{2,1,0:T(8,128)}) %all-reduce.5.cloned.1.call-update) | async-done | bytes 65552
  731.3 1.3 constant_dynamic-slice_fusion
  (223 shorter events, 45.1 us)
Async XLA Ops:
  7.2 724.2 %all-reduce.5.cloned.1.call-start = ((), (), s32[]{:S(2)}) async-start(), calls=%async_computation | async-start | bytes 131072
  300.9 10.6 %collective-permute-start = (f32[1,32,4,128]{3,1,2,0:T(8,128)S(1)}, f32[1,32,4,128]{3,1,2,0:T(8,128)S(1)}, u32[]{:S(2)}, u32[]{:S(2)}) collective-permute-start(f32[1,32,4,128]{3,1,2,0:T(8,128)S(1)} %get-tuple-element.186), channel_id=1, source_target_pairs={{0,16},{16,32},{32,48},{48,64},{64,80},{80,96},{96,112},{112,128},... | collective-permute-start | bytes 196616 | tf_op jit(solution)/shard_map/ppermute | solution.py:17
  302.7 8.8 %collective-permute-start.1 = (f32[1,32,4,128]{3,1,2,0:T(8,128)S(1)}, f32[1,32,4,128]{3,1,2,0:T(8,128)S(1)}, u32[]{:S(2)}, u32[]{:S(2)}) collective-permute-start(f32[1,32,4,128]{3,1,2,0:T(8,128)S(1)} %get-tuple-element.187), channel_id=1, source_target_pairs={{16,0},{32,16},{48,32},{64,48},{80,64},{96,80},{112,96},{128,112},... | collective-permute-start | bytes 196616 | tf_op jit(solution)/shard_map/ppermute | solution.py:19
  311.5 18.3 %collective-permute-start.2 = (f32[4,32,1,128]{3,1,2,0:T(8,128)S(1)}, f32[4,32,1,128]{3,1,2,0:T(8,128)S(1)}, u32[]{:S(2)}, u32[]{:S(2)}) collective-permute-start(f32[4,32,1,128]{3,1,2,0:T(8,128)S(1)} %get-tuple-element.182), channel_id=1, source_target_pairs={{0,1},{1,2},{2,3},{3,4},{4,5},{5,6},{6,7},{7,8},{8,9},{9,10},{10,1... | collective-permute-start | bytes 196616 | tf_op jit(solution)/shard_map/ppermute | solution.py:17
  325.5 5.6 collective-permute-start.3
  395.1 28.6 %collective-permute-start.4 = (f32[8,1,32,4,128]{4,0,3,2,1:T(8,128)S(1)}, f32[8,1,32,4,128]{4,0,3,2,1:T(8,128)S(1)}, u32[]{:S(2)}, u32[]{:S(2)}) collective-permute-start(f32[8,1,32,4,128]{4,0,3,2,1:T(8,128)S(1)} %get-tuple-element.100), channel_id=1, source_target_pairs={{0,16},{16,32},{32,48},{48,64},{64,80},{80,96},{96,112},{112,128},... | collective-permute-start | bytes 1572872 | tf_op jit(solution)/shard_map/ppermute | solution.py:17
  400.9 22.8 %collective-permute-start.5 = (f32[8,1,32,4,128]{4,0,3,2,1:T(8,128)S(1)}, f32[8,1,32,4,128]{4,0,3,2,1:T(8,128)S(1)}, u32[]{:S(2)}, u32[]{:S(2)}) collective-permute-start(f32[8,1,32,4,128]{4,0,3,2,1:T(8,128)S(1)} %get-tuple-element.101), channel_id=1, source_target_pairs={{16,0},{32,16},{48,32},{64,48},{80,64},{96,80},{112,96},{128,112},... | collective-permute-start | bytes 1572872 | tf_op jit(solution)/shard_map/ppermute | solution.py:19
  424.7 11.6 %collective-permute-start.6 = (f32[8,4,32,1,128]{4,0,3,2,1:T(8,128)}, f32[8,4,32,1,128]{4,0,3,2,1:T(8,128)S(1)}, u32[]{:S(2)}, u32[]{:S(2)}) collective-permute-start(f32[8,4,32,1,128]{4,0,3,2,1:T(8,128)} %get-tuple-element.98), channel_id=1, source_target_pairs={{0,1},{1,2},{2,3},{3,4},{4,5},{5,6},{6,7},{7,8},{8,9},{9,10},{10,1... | collective-permute-start | bytes 1572872 | tf_op jit(solution)/shard_map/ppermute | solution.py:17
  426.6 10.7 %collective-permute-start.7 = (f32[8,4,32,1,128]{4,0,3,2,1:T(8,128)}, f32[8,4,32,1,128]{4,0,3,2,1:T(8,128)S(1)}, u32[]{:S(2)}, u32[]{:S(2)}) collective-permute-start(f32[8,4,32,1,128]{4,0,3,2,1:T(8,128)} %get-tuple-element.99), channel_id=1, source_target_pairs={{1,0},{2,1},{3,2},{4,3},{5,4},{6,5},{7,6},{8,7},{9,8},{10,9},{11,1... | collective-permute-start | bytes 1572872 | tf_op jit(solution)/shard_map/ppermute | solution.py:19
  432.3 5.5 copy-start.61
  433.8 6.5 copy-start.57
  433.8 6.5 copy-start.60
  440.2 5.7 copy-start.58
  445.9 3.3 copy-start.41
  449.1 3.5 copy-start.31
  449.1 3.5 copy-start.32
  449.1 3.5 copy-start.33
  449.1 3.5 copy-start.34
  449.1 3.5 copy-start.35
  449.2 3.5 copy-start.36
  449.2 3.5 copy-start.37
  449.2 3.5 copy-start.38
  449.2 3.5 copy-start.40
  452.5 3.6 copy-start.20
  452.5 3.6 copy-start.23
  452.5 3.6 copy-start.24
  452.5 3.6 copy-start.26
  452.5 3.6 copy-start.27
  452.6 3.6 copy-start.28
  452.6 3.6 copy-start.29
  452.6 3.6 copy-start.30
  452.6 3.6 copy-start.59
  456.0 3.7 copy-start.11
  456.0 3.7 copy-start.12
  456.0 3.7 copy-start.13
  456.0 3.7 copy-start.14
  456.0 3.7 copy-start.15
  456.0 3.7 copy-start.16
  456.0 3.7 copy-start.17
  456.0 3.7 copy-start.18
  456.0 3.7 copy-start.39
  459.5 3.5 copy-start.25
  459.5 3.5 copy-start.48
  459.5 3.5 copy-start.49
  459.6 3.5 copy-start.50
  459.6 3.5 copy-start.51
  459.6 3.5 copy-start.52
  459.6 3.5 copy-start.53
  459.6 3.5 copy-start.54
  459.6 3.5 copy-start.55
  462.9 4.3 copy-start
  462.9 4.3 copy-start.1
  463.0 4.3 copy-start.2
  463.0 4.3 copy-start.21
  463.0 4.3 copy-start.22
  467.2 4.2 copy-start.3
  467.2 4.2 copy-start.4
  467.2 4.2 copy-start.5
  467.2 4.2 copy-start.6
  467.2 4.2 copy-start.7
  467.2 4.2 copy-start.8
  467.2 4.2 copy-start.9
  467.2 4.2 copy-start.10
  467.2 4.2 copy-start.19
  (7 other events, 23.4 us)
Sparse Core Ops, SparseCore 0:
  607.9 123.3 all-reduce.4
where the time goes:
time: 750 us; the launch traced here: 740 us
  blocking collectives  482 us (64%)
  waiting for transfers between devices  79.8 us (11%)
  local copies, waits for them, and re-layouts  71 us (9%)
  other arithmetic  57.4 us (8%)
  starting transfers between devices  32.6 us (4%)
  between operations  16.4 us (2%)
    psum x2, blocking collectives, dual_norms(): mass_a = lax.psum(jnp.sum(jnp.exp(values - top_a), axis=(0, 1)), 'aa')  124 us
    pmax x2, blocking collectives, dual_norms(): top_a = lax.pmax(jnp.max(values, axis=(0, 1)), 'aa')  120 us
    pmax x2, blocking collectives, dual_norms(): top_b = lax.pmax(jnp.max(values, axis=(2, 3)), 'ba')  79.7 us
    all_gather x1, blocking collectives, local(): rows_b = lax.all_gather(features_b, 'aa', axis=1, tiled=True)  70.3 us
    unnamed x2, waiting for transfers between devices  60.5 us
    psum x2, blocking collectives, dual_norms(): lax.psum(jnp.sum(jnp.exp(values - top_b[:, :, None, None]), axis=(2, 3)),...  54.3 us
    slice x85, local copies, waits for them, and re-layouts, spread_taps(): padded[offsets[0]:offsets[0] + extent[0], offsets[1]:offsets[1] + extent[...  51.1 us
    reduce_sum x11, other arithmetic, reduce_taps(): jnp.sum(kernel[:, offsets[0], offsets[1], offsets[2], offsets[3]].reshape...  35.4 us
  transfers between devices with their start and end apart: 9, of which 4 were waited for; matrix products, arithmetic and copies ran while one was open for 3% of the time, Pallas kernels for 0%

commit v1 on v0

v1 whole, which is shorter than its diff:
```python
import math

import jax
import jax.numpy as jnp
from jax import lax
from jax.experimental import pallas as pl
from jax.experimental.pallas import tpu as pltpu
from jax.sharding import PartitionSpec as P

F32, BF16, I32 = jnp.float32, jnp.bfloat16, jnp.int32
MESH = pl.DeviceIdType.MESH
OFFSET = math.log(64 * 32 * 64 * 128)
FAR = 1e30

AA_STEPS = sorted(
    [(dz, dx) for dz in range(-7, 9) for dx in range(2) if dz or dx],
    key=lambda o: -(abs(o[0]) + 2 * o[1]),
)
BA_STEPS = [15, 14, 13, 12, 11, 10, 9, 8, 7, 6, 5, 4, 3, 2, 1]
NEAR = [1, -1, 2, -2, 3, -3, 4, -4]


def iota(shape, dim):
    return lax.broadcasted_iota(I32, shape, dim)


def div(x, by):
    return (x * {3: 21846, 9: 7282, 27: 2428, 48: 1366}[by]) >> 16


def one_hot(mask):
    return jnp.where(mask, 1.0, 0.0).astype(BF16)


def dot(a, b):
    return jnp.dot(a, b, preferred_element_type=F32)


def dot_nt(a, b):
    return lax.dot_general(a, b, (((1,), (1,)), ((), ())), preferred_element_type=F32)


def halves(x):
    high = x.astype(BF16)
    return high, (x - high.astype(F32)).astype(BF16)


def select(chosen, x):
    high, low = halves(x)
    return dot(chosen, high) + dot(chosen, low)


def to_row(column):
    wide = jnp.broadcast_to(column, (64, 128))
    return jnp.concatenate([wide, wide], axis=0).T[0:1, 0:64]


def to_column(row):
    return jnp.broadcast_to(row, (128, 128)).T[0:64, 0:1]


def masses(cells):
    top_c = jnp.max(cells, axis=0, keepdims=True)
    lse_c = top_c + jnp.log(jnp.sum(jnp.exp(cells - top_c), axis=0, keepdims=True))
    top_r = jnp.max(cells, axis=1, keepdims=True)
    share = jnp.exp(cells - top_r)
    sum_r = jnp.sum(share, axis=1, keepdims=True)
    return lse_c, top_r, sum_r, share


def join(parts):
    top = jnp.max(parts, axis=0)
    return top + jnp.log(jnp.sum(jnp.exp(parts - top[None]), axis=0))


def kernel(
    pa, pb, wts, lm, warped,
    ga, gb, ax, bx, perm_b, w1f, w1, w2f, w2,
    na_src, nb_src, na_all, nb_all, na_own, nb_own, na_lo, na_hi, nb_lo, nb_hi,
    own, sx, xt, x3, x3_low, zs, ft, rn, pn, ps, pr,
    na2_src, nb2_src, na2_all, nb2_all, nar,
    s_a, r_a, s_b, r_b, s_h, r_h, s_na, r_na, s_nb, r_nb, s_na2, r_na2, s_nb2, r_nb2, s_p, r_p,
):
    me_a, me_b = lax.axis_index("aa"), lax.axis_index("ba")
    z, xh = me_a >> 1, me_a & 1

    def at(dz, dx=0):
        return ((((z + dz) & 15) << 1) | ((xh + dx) & 1), me_b)

    def send(src, dst, s, r, to):
        copy = pltpu.make_async_remote_copy(
            src_ref=src, dst_ref=dst, send_sem=s, recv_sem=r, device_id=to, device_id_type=MESH
        )
        copy.start()
        pending.append(copy)

    def arrived(ref, r):
        pltpu.make_async_remote_copy(
            src_ref=ref, dst_ref=ref, send_sem=r, recv_sem=r, device_id=at(0, 1), device_id_type=MESH
        ).wait_recv()

    pending = []

    barrier = pltpu.get_barrier_semaphore()
    greet = [at(d) for d in NEAR] + [at(0, 1), at(4, 1), at(-4, 1)]
    greet += [(me_a, (me_b + d) & 15) for d in BA_STEPS]
    for peer in greet:
        pl.semaphore_signal(barrier, inc=1, device_id=peer, device_id_type=MESH)

    ga[pl.ds(me_b, 1)] = pa[...][None]
    gb[pl.ds(me_a, 1)] = pb[...][None]
    row = iota((512, 128), 0)
    src = ((row >> 2) & 31) * 16 + (row >> 7) * 4 + (row & 3)
    for g in range(4):
        perm_b[:, g * 128 : (g + 1) * 128] = one_hot(src == iota((512, 128), 1) + g * 128)
    row = iota((64, 256), 0)
    perm_a = one_hot(((row & 31) >> 1) * 16 + (row >> 5) * 2 + (row & 1) == iota((64, 256), 1))

    pl.semaphore_wait(barrier, len(greet))

    for k, d in enumerate(NEAR):
        send(pb, gb.at[me_a], s_b.at[k], r_b.at[me_a], at(d))
    send(pb, gb.at[me_a], s_b.at[8], r_b.at[me_a], at(0, 1))
    for k, d in enumerate(BA_STEPS):
        send(pa, ga.at[me_b], s_a.at[k], r_a.at[me_b], (me_a, (me_b + d) & 15))

    col = iota((8, 512), 1)
    d24 = div(col, 48)
    rest = col - 48 * d24
    a1, b1 = rest >> 3, rest & 7
    d2 = (d24 * 11) >> 5
    tap = a1 * 27 + d2 * 9 + b1 * 3 + (d24 - 3 * d2)
    tap = jnp.where((a1 < 3) & (b1 < 3) & (col < 432), tap, -1)
    spread = one_hot(iota((128, 512), 0) == jnp.broadcast_to(tap[0:1], (128, 512)))
    high, low = halves(wts[:, 0:128])
    base = dot(high, spread) + dot(low, spread)
    for p in range(24):
        s = (p // 6) * 8 + p % 6
        w1f[p * 8 : p * 8 + 8] = pltpu.roll(base, s, 1) if s else base
    w1[0:192], w1[192:384] = halves(w1f[:, 0:432])

    k, c = iota((128, 256), 0), iota((128, 256), 1)
    k3, k9, k27 = div(k, 3), div(k, 9), div(k, 27)
    ca = div(c, 48)
    cb = (c - 48 * ca) >> 3
    pick = one_hot(iota((8, 256), 0) == (iota((8, 256), 1) & 7))
    taps = sum(
        lax.dot_general(part, pick, (((0,), (0,)), ((), ())), preferred_element_type=F32)
        for part in halves(wts[:, 128:256])
    )
    taps = jnp.where((k27 == ca) & (k3 - 3 * k9 == cb), taps, 0.0)
    k = iota((16, 128), 1)
    k3, k9, k27 = div(k, 3), div(k, 9), div(k, 27)
    place = one_hot(iota((16, 128), 0) == (k9 - 3 * k27) * 3 + (k - 3 * k3))
    base = select(place, taps)
    for o in range(8):
        s = (o // 4) * 48 + (o % 4) * 8
        w2f[o * 16 : o * 16 + 16] = pltpu.roll(base, s, 1) if s else base
    r, c = iota((72, 128), 0), iota((72, 128), 1)
    order = one_hot(c == (r & 7) * 16 + (r >> 3))
    c = iota((72, 256), 1)
    ca = div(c, 48)
    cb = (c - 48 * ca) >> 3
    ra, rb = 2 * me_a - 1 + ca, 4 * me_b - 1 + cb
    inside = (ra >= 0) & (ra < 64) & (rb >= 0) & (rb < 64)
    w2[0:72], w2[72:144] = halves(jnp.where(inside, select(order, w2f[...]), 0.0))
    bias = wts[:, 256:384]
    bias = jnp.concatenate([jnp.concatenate([bias] * 24, axis=0)] * 4, axis=1)
    for x in (x3, x3_low):
        x[:, 0:128] = jnp.zeros((144, 128), BF16)
        x[:, 33 * 128 :] = jnp.zeros((144, 128), BF16)
    zs[:, 0:128] = jnp.zeros((72, 128), F32)
    zs[:, 33 * 128 :] = jnp.zeros((72, 128), F32)
    nb_src[...] = jnp.zeros((1, 128), F32)
    nb2_src[...] = jnp.zeros((1, 128), F32)
    ps[...] = jnp.zeros((256, 128), F32)

    n = 9
    for d in NEAR:
        slot = at(d)[0]
        arrived(gb.at[slot], r_b.at[slot])
        targets = [at(0, 1)]
        if d != 4:
            targets = [at(-4 if d > 0 else 4, 1), at(-4 if d > 0 else 4), at(0, 1)]
        for to in targets:
            send(gb.at[slot], gb.at[slot], s_b.at[n], r_b.at[slot], to)
            n += 1
    for d in BA_STEPS:
        slot = (me_b + d) & 15
        arrived(ga.at[slot], r_a.at[slot])
    ax[64:128] = dot(perm_a, ga[...].reshape(256, 256)).astype(BF16)
    for d, dx in reversed(AA_STEPS):
        if dx or abs(d) > 4:
            slot = at(d, dx)[0]
            arrived(gb.at[slot], r_b.at[slot])
    bx[256:768] = dot(perm_b[...], gb[...].reshape(512, 256)).astype(BF16)

    up_a, down_a = ((me_a + 1) & 31, me_b), ((me_a - 1) & 31, me_b)
    up_b, down_b = (me_a, (me_b + 1) & 15), (me_a, (me_b - 1) & 15)
    send(bx.at[512:768], bx.at[0:256], s_h.at[0], r_h.at[0], up_b)
    send(bx.at[256:512], bx.at[768:1024], s_h.at[1], r_h.at[1], down_b)
    send(ax.at[64:128], ax.at[0:64], s_h.at[2], r_h.at[2], up_a)
    send(ax.at[64:128], ax.at[128:192], s_h.at[3], r_h.at[3], down_a)

    scores = dot_nt(ax[64:128], bx[256:768]) * (1.0 / 16.0)
    own[...] = scores
    lse_c, top_r, sum_r, _ = masses(scores)
    for b in range(4):
        na_src[b : b + 1] = lse_c[:, b * 128 : (b + 1) * 128]
    nb_src[:, 0:64] = to_row(top_r + jnp.log(sum_r))
    for k, (dz, dx) in enumerate(AA_STEPS):
        send(na_src, na_all.at[me_a], s_na.at[k], r_na.at[me_a], at(dz, dx))
    for k, d in enumerate(BA_STEPS):
        send(nb_src, nb_all.at[me_b], s_nb.at[k], r_nb.at[me_b], (me_a, (me_b + d) & 15))
    na_all[pl.ds(me_a, 1)] = na_src[...][None]
    nb_all[pl.ds(me_b, 1)] = nb_src[...][None]

    arrived(bx.at[0:256], r_h.at[0])
    arrived(bx.at[768:1024], r_h.at[1])
    arrived(ax.at[0:64], r_h.at[2])
    arrived(ax.at[128:192], r_h.at[3])
    for t in range(3):
        sx[t * 64 : t * 64 + 64] = dot_nt(ax[t * 64 : t * 64 + 64], bx[...]) * (1.0 / 8.0)

    for d in BA_STEPS:
        slot = (me_b + d) & 15
        arrived(nb_all.at[slot], r_nb.at[slot])
    nb_own[...] = join(nb_all[...])
    send(nb_own, nb_lo, s_h.at[4], r_h.at[4], up_a)
    send(nb_own, nb_hi, s_h.at[5], r_h.at[5], down_a)
    for dz, dx in reversed(AA_STEPS):
        slot = at(dz, dx)[0]
        arrived(na_all.at[slot], r_na.at[slot])
    na_own[...] = join(na_all[...])
    send(na_own, na_lo, s_h.at[6], r_h.at[6], up_b)
    send(na_own, na_hi, s_h.at[7], r_h.at[7], down_b)
    arrived(nb_lo, r_h.at[4])
    arrived(nb_hi, r_h.at[5])
    cols = [
        to_column(jnp.where(me_a > 0, nb_lo[...], FAR)),
        to_column(nb_own[...]),
        to_column(jnp.where(me_a < 31, nb_hi[...], FAR)),
    ]
    arrived(na_lo, r_h.at[6])
    arrived(na_hi, r_h.at[7])
    nar[0:2] = jnp.where(me_b > 0, na_lo[2:4], FAR) - OFFSET
    nar[2:6] = na_own[...] - OFFSET
    nar[6:8] = jnp.where(me_b < 15, na_hi[0:2], FAR) - OFFSET

    for t in range(3):
        for b in range(8):
            v = sx[t * 64 : t * 64 + 64, b * 128 : (b + 1) * 128] - cols[t] - nar[b : b + 1]
            v = jnp.maximum(v, 0.0) + jnp.log(1.0 + jnp.exp(-jnp.abs(v)))
            xt[pl.ds(t * 512 + b, 64, stride=8), :] = v
    lane = iota((48, 128), 1)
    for a2 in range(32):
        rows = [xt[pl.ds(((t * 2 + a) * 32 + a2) * 8, 8), :] for t in range(3) for a in range(2)]
        m = jnp.concatenate(rows, axis=0)
        out = slice((a2 + 1) * 128, (a2 + 2) * 128)
        x3[0:48, out], x3_low[0:48, out] = halves(jnp.where(lane > 0, pltpu.roll(m, 1, 1), 0.0))
        x3[48:96, out], x3_low[48:96, out] = halves(m)
        x3[96:144, out], x3_low[96:144, out] = halves(jnp.where(lane < 127, pltpu.roll(m, 127, 1), 0.0))
    for g in range(8):
        at2 = g * 512
        high, low = (
            jnp.concatenate([x[:, at2 + d * 128 : at2 + d * 128 + 512] for d in range(3)], axis=0)
            for x in (x3, x3_low)
        )
        hidden = dot(w1[...], high)
        hidden = hidden[0:192] + hidden[192:384] + dot(w1[0:192], low)
        high, low = halves(jnp.maximum(hidden + bias, 0.0))
        out = dot(w2[:, 0:192], high)
        zs[:, at2 + 128 : at2 + 640] = out[0:72] + out[72:144] + dot(w2[0:72, 0:192], low)
    lane = iota((8, 128), 1)
    for a2 in range(32):
        u = []
        for d4 in range(3):
            terms = [
                zs[(d * 3 + d4) * 8 : (d * 3 + d4) * 8 + 8, (a2 + d) * 128 : (a2 + d + 1) * 128]
                for d in range(3)
            ]
            u.append(terms[0] + terms[1] + terms[2])
        f = u[1] + jnp.where(lane > 0, pltpu.roll(u[0], 1, 1), 0.0)
        f = f + jnp.where(lane < 127, pltpu.roll(u[2], 127, 1), 0.0)
        ft[a2 * 8 : a2 * 8 + 8] = jnp.maximum(f, 0.0)
    for a in range(2):
        for b in range(4):
            rows, lanes = slice(a * 32, a * 32 + 32), slice(b * 128, (b + 1) * 128)
            rn[rows, lanes] = own[rows, lanes] + ft[pl.ds(a * 4 + b, 32, stride=8), :]

    refined = rn[...]
    lse_c, top_r, sum_r, share = masses(refined)
    for b in range(4):
        na2_src[b : b + 1] = lse_c[:, b * 128 : (b + 1) * 128]
    for k, (dz, dx) in enumerate(AA_STEPS):
        send(na2_src, na2_all.at[me_a], s_na2.at[k], r_na2.at[me_a], at(dz, dx))
    lse_r = top_r + jnp.log(sum_r)
    nb2_src[:, 0:64] = to_row(lse_r)
    for k, d in enumerate(BA_STEPS):
        send(nb2_src, nb2_all.at[me_b], s_nb2.at[k], r_nb2.at[me_b], (me_a, (me_b + d) & 15))
    na2_all[pl.ds(me_a, 1)] = na2_src[...][None]
    nb2_all[pl.ds(me_b, 1)] = nb2_src[...][None]
    high, low = halves(share)
    features = bx[256:768]
    moved = (dot(high, features) + dot(low, features)) / sum_r
    pn[0:64] = moved[:, 0:128]
    pn[64:128] = moved[:, 128:256]
    pn[128:192] = jnp.broadcast_to(lse_r, (64, 128))
    for g in range(3):
        for q in range(4):
            rows = pl.ds(g * 64 + (q >> 1) * 32 + (q & 1), 16, stride=2)
            ps[pl.ds(g * 4 + q, 16, stride=16), :] = pn[rows, :]
    for k, d in enumerate(BA_STEPS):
        to = (me_b + d) & 15
        block = ps.at[pl.ds(pl.multiple_of(to * 16, 16), 16)]
        send(block, pr.at[me_b], s_p.at[k], r_p.at[me_b], (me_a, to))
    pr[pl.ds(me_b, 1)] = ps[pl.ds(pl.multiple_of(me_b * 16, 16), 16), :][None]

    for d in BA_STEPS:
        slot = (me_b + d) & 15
        arrived(nb2_all.at[slot], r_nb2.at[slot])
    col = to_column(join(nb2_all[...])) - OFFSET
    for d in BA_STEPS:
        slot = (me_b + d) & 15
        arrived(pr.at[slot], r_p.at[slot])
    lse = pr[:, 8:12, :]
    weight = jnp.exp(lse - jnp.max(lse, axis=0, keepdims=True))
    total = jnp.sum(weight, axis=0)
    warped[:, 0:128] = jnp.sum(weight * pr[:, 0:4, :], axis=0) / total
    warped[:, 128:256] = jnp.sum(weight * pr[:, 4:8, :], axis=0) / total
    twice = 2.0 * refined - col
    for dz, dx in reversed(AA_STEPS):
        slot = at(dz, dx)[0]
        arrived(na2_all.at[slot], r_na2.at[slot])
    norm = join(na2_all[...])
    for b in range(4):
        lm[pl.ds(b, 64, stride=4), :] = twice[:, b * 128 : (b + 1) * 128] - norm[b : b + 1]
    for copy in pending:
        copy.wait_send()


def local(features_a, features_b, conv_in, bias_in, conv_out):
    pa = jnp.pad(features_a.reshape(4, 256), ((0, 12), (0, 0)))
    pb = features_b.reshape(16, 256)
    wts = jnp.concatenate(
        [
            jnp.pad(conv_in.reshape(8, 81), ((0, 0), (0, 47))),
            jnp.pad(conv_out.reshape(8, 81), ((0, 0), (0, 47))),
            jnp.broadcast_to(bias_in[:, None], (8, 128)),
        ],
        axis=1,
    )
    dma = pltpu.SemaphoreType.DMA
    vmem = pltpu.VMEM
    lm, warped = pl.pallas_call(
        kernel,
        out_shape=(jax.ShapeDtypeStruct((256, 128), F32), jax.ShapeDtypeStruct((4, 256), F32)),
        in_specs=[pl.BlockSpec(memory_space=pltpu.VMEM)] * 3,
        out_specs=(pl.BlockSpec(memory_space=pltpu.VMEM),) * 2,
        scratch_shapes=[
            vmem((16, 16, 256), BF16), vmem((32, 16, 256), BF16),
            vmem((192, 256), BF16), vmem((1024, 256), BF16), vmem((512, 512), BF16),
            vmem((192, 512), F32), vmem((384, 432), BF16), vmem((128, 256), F32), vmem((144, 256), BF16),
            vmem((4, 128), F32), vmem((1, 128), F32), vmem((32, 4, 128), F32), vmem((16, 1, 128), F32),
            vmem((4, 128), F32), vmem((1, 128), F32), vmem((4, 128), F32), vmem((4, 128), F32),
            vmem((1, 128), F32), vmem((1, 128), F32),
            vmem((64, 512), F32), vmem((192, 1024), F32), vmem((1536, 128), F32),
            vmem((144, 34 * 128), BF16), vmem((144, 34 * 128), BF16), vmem((72, 34 * 128), F32), vmem((256, 128), F32),
            vmem((64, 512), F32), vmem((192, 128), F32), vmem((256, 128), F32), vmem((16, 16, 128), F32),
            vmem((4, 128), F32), vmem((1, 128), F32), vmem((32, 4, 128), F32), vmem((16, 1, 128), F32),
            vmem((8, 128), F32),
            dma((15,)), dma((16,)), dma((31,)), dma((32,)), dma((8,)), dma((8,)),
            dma((31,)), dma((32,)), dma((15,)), dma((16,)),
            dma((31,)), dma((32,)), dma((15,)), dma((16,)), dma((15,)), dma((16,)),
        ],
        compiler_params=pltpu.CompilerParams(
            collective_id=0, has_side_effects=True, vmem_limit_bytes=40 * 2**20
        ),
        cost_estimate=pl.CostEstimate(flops=2 * 10**9, bytes_accessed=10**6, transcendentals=10**6),
    )(pa, pb, wts)
    return lm.reshape(2, 32, 4, 128), warped.reshape(2, 2, 256)


def solution(mesh):
    placed = (P("aa", "ba", None), P("ba", "aa", None), P(), P(), P())
    return jax.shard_map(
        local,
        mesh=mesh,
        in_specs=placed,
        out_specs=(P("aa", None, "ba", None), P("aa", "ba", None)),
        check_vma=False,
    )
```

time: 750 us -> 59.6 us (0.08); the launches traced: 740 us -> 59.4 us
  blocking collectives: 482 us -> 0 us
  waiting for transfers between devices: 79.8 us -> 0 us
  local copies, waits for them, and re-layouts: 71 us -> 3.67 us
  other arithmetic: 57.4 us -> 0.01 us
  Pallas kernels: 0 us -> 55.1 us
  starting transfers between devices: 32.6 us -> 0 us
  between operations: 16.4 us -> 0.66 us
    pmax x4 -> x0, blocking collectives: 200 us -> none  [the longest x2 120 us: dual_norms(): top_a = lax.pmax(jnp.max(values, axis=(0, 1)), 'aa')]
    psum x4 -> x0, blocking collectives: 178 us -> none  [the longest x2 124 us: dual_norms(): mass_a = lax.psum(jnp.sum(jnp.exp(values - top_a), axis=(0, 1)), 'aa')]
    all_gather x2 -> x0, blocking collectives: 104 us -> none  [the longest x1 70.3 us: local(): rows_b = lax.all_gather(features_b, 'aa', axis=1, tiled=True)]
    unnamed x2 -> x0, waiting for transfers between devices: 60.5 us -> none
    pallas_call x0 -> x1, Pallas kernels: none -> 55.1 us  [local(): pl.pallas_call(kernel, out_shape=(jax.ShapeDtypeStruct((256, 128), F32),...]
    slice x87 -> x0, local copies, waits for them, and re-layouts: 51.2 us -> none  [the longest x85 51.1 us: spread_taps(): padded[offsets[0]:offsets[0] + extent[0], offsets[1]:offsets[1] + extent[...]
    reduce_sum x14 -> x0, other arithmetic: 35.9 us -> none  [the longest x11 35.4 us: reduce_taps(): jnp.sum(kernel[:, offsets[0], offsets[1], offsets[2], offsets[3]].reshape...]
    ppermute x8 -> x0, starting transfers between devices: 32.6 us -> none  [the longest x4 23.5 us: padded_2(): lax.ppermute(tail, axis, [(i, (i + 1) % count) for i in range(ends)])]
  transfers between devices with their start and end apart: 9 -> 0, of which waited for: 4 -> 0; matrix products, arithmetic and copies ran while one was open for 3% -> 0% of each run, Pallas kernels for 0% -> 0%
where the time goes in v1:
time: 59.6 us; the launch traced here: 59.4 us
  Pallas kernels  55.1 us (92%)
  local copies, waits for them, and re-layouts  3.67 us (6%)
  between operations  0.66 us (1%)
    pallas_call x1, Pallas kernels, local(): pl.pallas_call(kernel, out_shape=(jax.ShapeDtypeStruct((256, 128), F32),...  55.1 us
    unnamed x7, local copies, waits for them, and re-layouts  1.28 us

profile of v1, /device:TPU:1, one launch (start us, length us, event | category | flops | bytes accessed | tf_op | source)
XLA Modules:
  0.0 59.4 jit_solution(15727045801286231243)
XLA Ops:
  0.6 0.0 copy-start.2
  0.6 0.7 %reshape.23 = bf16[4,256]{1,0:T(4,128)(2,1)S(1)} reshape(bf16[2,2,256]{2,1,0:T(2,128)(2,1)} %param.5) | data formatting | bytes 4096 | tf_op jit(solution)/shard_map/reshape | solution.py:343
  1.3 0.0 copy-done.2
  1.3 0.0 copy-start.1
  1.3 0.1 broadcast_in_dim.2
  1.4 0.6 %copy-done.1 = bf16[4,4,256]{2,1,0:T(4,128)(2,1)S(1)} copy-done((bf16[4,4,256]{2,1,0:T(4,128)(2,1)S(1)}, bf16[4,4,256]{2,1,0:T(4,128)(2,1)}, u32[]{:S(2)}) %copy-start.1) | copy-done | bytes 8216
  2.0 0.0 copy-start
  2.0 0.8 %reshape.25 = f32[8,81]{0,1:T(8,128)S(1)} reshape(f32[8,3,3,3,3]{0,4,3,2,1:T(4,128)} %param.7) | data formatting | bytes 5184 | tf_op jit(solution)/shard_map/reshape | solution.py:347
  2.9 0.1 copy.9
  3.0 0.0 copy-done
  3.0 0.1 copy.10
  3.1 55.1 %shard_map.68 = (f32[256,128]{1,0:T(8,128)S(1)}, f32[4,256]{1,0:T(4,128)S(1)}) custom-call(bf16[16,256]{1,0:T(8,128)(2,1)S(1)} %pad.11.pa, bf16[16,256]{1,0:T(8,128)(2,1)S(1)} %reshape.24.pb, f32[8,384]{1,0:T(8,128)S(1)} %fusion.wts), custom_call_target="tpu_custom_call" | custom-call | flops 2000000000 | bytes 1000000 | tf_op jit(solution)/shard_map/pallas_call | solution.py:355
  58.2 0.6 %reshape.28 = f32[2,2,256]{2,1,0:T(2,128)} reshape(f32[4,256]{1,0:T(4,128)S(1)} %get-tuple-element.5) | data formatting | bytes 8192 | tf_op jit(solution)/shard_map/reshape | solution.py:381
  58.8 0.7 %copy.12 = f32[2,32,4,128]{3,2,1,0:T(4,128)} copy(f32[2,32,4,128]{3,2,1,0:T(4,128)S(1)} %bitcast.5) | data formatting | bytes 262144
  (4 shorter events, 0.0 us)
Async XLA Ops:
  0.6 0.7 %copy-start.2 = (f32[8]{0:T(128)S(1)}, f32[8]{0:T(128)}, u32[]{:S(2)}) copy-start(f32[8]{0:T(128)} %param.8) | copy-start | bytes 100
  1.3 0.7 %copy-start.1 = (bf16[4,4,256]{2,1,0:T(4,128)(2,1)S(1)}, bf16[4,4,256]{2,1,0:T(4,128)(2,1)}, u32[]{:S(2)}) copy-start(bf16[4,4,256]{2,1,0:T(4,128)(2,1)} %param.6) | copy-start | bytes 24580
  2.0 0.9 %copy-start = (f32[8,3,3,3,3]{0,4,3,2,1:T(4,128)S(1)}, f32[8,3,3,3,3]{0,4,3,2,1:T(4,128)}, u32[]{:S(2)}) copy-start(f32[8,3,3,3,3]{0,4,3,2,1:T(4,128)} %param.9) | copy-start | bytes 7780

commit v2 on v1

v2 whole, which is shorter than its diff:
```python
import math

import jax
import jax.numpy as jnp
from jax import lax
from jax.experimental import pallas as pl
from jax.experimental.pallas import tpu as pltpu
from jax.sharding import PartitionSpec as P

F32, BF16, I32 = jnp.float32, jnp.bfloat16, jnp.int32
MESH = pl.DeviceIdType.MESH
OFFSET = math.log(64 * 32 * 64 * 128)
FAR = 1e30

AA_STEPS = sorted(
    [(dz, dx) for dz in range(-7, 9) for dx in range(2) if dz or dx],
    key=lambda o: -(abs(o[0]) + 2 * o[1]),
)
BA_STEPS = [15, 14, 13, 12, 11, 10, 9, 8, 7, 6, 5, 4, 3, 2, 1]
NEAR = [4, -4, 3, -3, 2, -2, 1, -1]


def iota(shape, dim):
    return lax.broadcasted_iota(I32, shape, dim)


def div(x, by):
    return (x * {3: 21846, 9: 7282, 27: 2428, 48: 1366}[by]) >> 16


def one_hot(mask):
    return jnp.where(mask, 1.0, 0.0).astype(BF16)


def dot(a, b):
    return jnp.dot(a, b, preferred_element_type=F32)


def dot_nt(a, b):
    return lax.dot_general(a, b, (((1,), (1,)), ((), ())), preferred_element_type=F32)


def halves(x):
    high = x.astype(BF16)
    return high, (x - high.astype(F32)).astype(BF16)


def select(chosen, x):
    high, low = halves(x)
    return dot(chosen, high) + dot(chosen, low)


def to_row(column):
    wide = jnp.broadcast_to(column, (64, 128))
    return jnp.concatenate([wide, wide], axis=0).T[0:1, 0:64]


def to_column(row):
    return jnp.broadcast_to(row, (128, 128)).T[0:64, 0:1]


def masses(cells):
    top_c = jnp.max(cells, axis=0, keepdims=True)
    lse_c = top_c + jnp.log(jnp.sum(jnp.exp(cells - top_c), axis=0, keepdims=True))
    top_r = jnp.max(cells, axis=1, keepdims=True)
    share = jnp.exp(cells - top_r)
    sum_r = jnp.sum(share, axis=1, keepdims=True)
    return lse_c, top_r, sum_r, share


def join(parts):
    top = jnp.max(parts, axis=0)
    return top + jnp.log(jnp.sum(jnp.exp(parts - top[None]), axis=0))


def kernel(
    fa_hbm, fb_hbm, ci_hbm, co_hbm, bias_hbm, lm, warped,
    fa, fb, ci, co, bias_row, stage, taps_m, pa, pb, ga, gb, ax, bx, perm_b, w1f, w1, w2f, w2,
    na_src, nb_src, na_all, nb_all, na_own, nb_own, na_lo, na_hi, nb_lo, nb_hi,
    own, sx, xt, x3, x3_low, zs, ft, rn, pn, ps, pr,
    na2_src, nb2_src, na2_all, nb2_all, nar,
    s_a, r_a, s_b, r_b, s_h, r_h, s_na, r_na, s_nb, r_nb, s_na2, r_na2, s_nb2, r_nb2, s_p, r_p, s_in,
):
    me_a, me_b = lax.axis_index("aa"), lax.axis_index("ba")
    z, xh = me_a >> 1, me_a & 1

    def at(dz, dx=0):
        return ((((z + dz) & 15) << 1) | ((xh + dx) & 1), me_b)

    def send(src, dst, s, r, to):
        copy = pltpu.make_async_remote_copy(
            src_ref=src, dst_ref=dst, send_sem=s, recv_sem=r, device_id=to, device_id_type=MESH
        )
        copy.start()

    def arrived(ref, r):
        pltpu.make_async_remote_copy(
            src_ref=ref, dst_ref=ref, send_sem=r, recv_sem=r, device_id=at(0, 1), device_id_type=MESH
        ).wait_recv()

    given = [
        pltpu.make_async_copy(src, dst, s_in.at[k])
        for k, (src, dst) in enumerate(
            [(fa_hbm, fa), (fb_hbm, fb), (ci_hbm, ci), (co_hbm, co), (bias_hbm, bias_row)]
        )
    ]
    for copy in given:
        copy.start()

    barrier = pltpu.get_barrier_semaphore()
    greet = [at(d, dx) for d in NEAR for dx in range(2)] + [at(0, 1)]
    greet += [(me_a, (me_b + d) & 15) for d in BA_STEPS]
    for peer in greet:
        pl.semaphore_signal(barrier, inc=1, device_id=peer, device_id_type=MESH)

    stage[0:16] = jnp.zeros((16, 256), F32)
    given[0].wait()
    for a in range(2):
        stage[a * 2 : a * 2 + 2] = fa[a].astype(F32)
    pa[...] = stage[0:16].astype(BF16)
    given[1].wait()
    for b in range(4):
        stage[16 + b * 4 : 20 + b * 4] = fb[b].astype(F32)
    pb[...] = stage[16:32].astype(BF16)
    ga[pl.ds(me_b, 1)] = pa[...][None]
    gb[pl.ds(me_a, 1)] = pb[...][None]
    pl.semaphore_wait(barrier, len(greet))
    for k, d in enumerate(NEAR):
        send(pb, gb.at[me_a], s_b.at[0], r_b.at[k], at(d))
    send(pb, gb.at[me_a], s_b.at[0], r_b.at[8], at(0, 1))
    for d in BA_STEPS:
        send(pa, ga.at[me_b], s_a.at[0], r_a.at[0], (me_a, (me_b + d) & 15))

    row = iota((512, 128), 0)
    src = ((row >> 2) & 31) * 16 + (row >> 7) * 4 + (row & 3)
    for g in range(4):
        perm_b[:, g * 128 : (g + 1) * 128] = one_hot(src == iota((512, 128), 1) + g * 128)
    row = iota((64, 256), 0)
    perm_a = one_hot(((row & 31) >> 1) * 16 + (row >> 5) * 2 + (row & 1) == iota((64, 256), 1))

    for d in reversed(NEAR):
        slot = at(d)[0]
        arrived(gb.at[slot], r_b.at[NEAR.index(-d)])
        targets = [at(0, 1)]
        if abs(d) == 4:
            away = [-4, -3, -2, -1] if d > 0 else [3, 2, 1]
            targets = [at(step, dx) for step in away for dx in (1, 0)] + targets
        for to in targets:
            send(gb.at[slot], gb.at[slot], s_b.at[0], r_b.at[8], to)
    arrived(ga.at[0:15], r_a.at[0])
    ax[64:128] = dot(perm_a, ga[...].reshape(256, 256)).astype(BF16)
    up_a, down_a = ((me_a + 1) & 31, me_b), ((me_a - 1) & 31, me_b)
    up_b, down_b = (me_a, (me_b + 1) & 15), (me_a, (me_b - 1) & 15)
    send(ax.at[64:128], ax.at[0:64], s_h.at[2], r_h.at[2], up_a)
    send(ax.at[64:128], ax.at[128:192], s_h.at[3], r_h.at[3], down_a)
    arrived(gb.at[0:23], r_b.at[8])
    bx[256:768] = dot(perm_b[...], gb[...].reshape(512, 256)).astype(BF16)

    send(bx.at[512:768], bx.at[0:256], s_h.at[0], r_h.at[0], up_b)
    send(bx.at[256:512], bx.at[768:1024], s_h.at[1], r_h.at[1], down_b)

    scores = dot_nt(ax[64:128], bx[256:768]) * (1.0 / 16.0)
    own[...] = scores
    lse_c, top_r, sum_r, _ = masses(scores)
    for b in range(4):
        na_src[b : b + 1] = lse_c[:, b * 128 : (b + 1) * 128]
    nb_src[...] = jnp.zeros((1, 128), F32)
    nb_src[:, 0:64] = to_row(top_r + jnp.log(sum_r))
    for dz, dx in AA_STEPS:
        send(na_src, na_all.at[me_a], s_na.at[0], r_na.at[0], at(dz, dx))
    for d in BA_STEPS:
        send(nb_src, nb_all.at[me_b], s_nb.at[0], r_nb.at[0], (me_a, (me_b + d) & 15))
    na_all[pl.ds(me_a, 1)] = na_src[...][None]
    nb_all[pl.ds(me_b, 1)] = nb_src[...][None]

    col = iota((8, 512), 1)
    d24 = div(col, 48)
    rest = col - 48 * d24
    a1, b1 = rest >> 3, rest & 7
    d2 = (d24 * 11) >> 5
    tap = (a1 * 9 + d2 * 3 + b1) * 8 + (d24 - 3 * d2)
    tap = jnp.where((a1 < 3) & (b1 < 3) & (col < 432), tap, -1)
    spread = one_hot(iota((256, 512), 0) == jnp.broadcast_to(tap[0:1], (256, 512)))
    taps_m[...] = jnp.zeros((512, 128), F32)
    for copy in given[2:]:
        copy.wait()
    for k in range(27):
        taps_m[k * 8 : k * 8 + 3, 0:8] = ci[k]
        taps_m[256 + k * 8 : 259 + k * 8, 0:8] = co[k]
    base = sum(
        lax.dot_general(part, spread, (((0,), (0,)), ((), ())), preferred_element_type=F32)
        for part in halves(taps_m[0:256])
    )[0:8]
    for p in range(24):
        s = (p // 6) * 8 + p % 6
        w1f[p * 8 : p * 8 + 8] = pltpu.roll(base, s, 1) if s else base
    w1[0:192], w1[192:384] = halves(w1f[:, 0:432])

    k, c = iota((256, 256), 0) >> 3, iota((256, 256), 1)
    k3 = (k * 11) >> 5
    k9 = div(k, 9)
    ca = div(c, 48)
    cb = (c - 48 * ca) >> 3
    pick = one_hot(iota((128, 256), 0) == (iota((128, 256), 1) & 7))
    high, low = halves(taps_m[256:512])
    taps = jnp.where((k9 == ca) & (k - 3 * k3 == cb), dot(high, pick) + dot(low, pick), 0.0)
    k = iota((16, 256), 1)
    k3, k9 = ((k >> 3) * 11) >> 5, div(k >> 3, 9)
    place = one_hot(iota((16, 256), 0) == (k3 - 3 * k9) * 3 + (k & 7))
    place = jnp.where((k & 7) < 3, place, jnp.zeros_like(place))
    base = select(place, taps)
    for o in range(8):
        s = (o // 4) * 48 + (o % 4) * 8
        w2f[o * 16 : o * 16 + 16] = pltpu.roll(base, s, 1) if s else base
    r, c = iota((72, 128), 0), iota((72, 128), 1)
    order = one_hot(c == (r & 7) * 16 + (r >> 3))
    c = iota((72, 256), 1)
    ca = div(c, 48)
    cb = (c - 48 * ca) >> 3
    ra, rb = 2 * me_a - 1 + ca, 4 * me_b - 1 + cb
    inside = (ra >= 0) & (ra < 64) & (rb >= 0) & (rb < 64)
    w2[0:72], w2[72:144] = halves(jnp.where(inside, select(order, w2f[...]), 0.0))
    bias = jnp.where(iota((8, 8), 0) == iota((8, 8), 1), bias_row[...], 0.0)
    bias = jnp.broadcast_to(jnp.sum(bias, axis=1, keepdims=True), (8, 128))
    bias = jnp.concatenate([jnp.concatenate([bias] * 24, axis=0)] * 4, axis=1)
    for x in (x3, x3_low):
        x[:, 0:128] = jnp.zeros((144, 128), BF16)
        x[:, 33 * 128 :] = jnp.zeros((144, 128), BF16)
    zs[:, 0:128] = jnp.zeros((72, 128), F32)
    zs[:, 33 * 128 :] = jnp.zeros((72, 128), F32)
    nb2_src[...] = jnp.zeros((1, 128), F32)
    ps[...] = jnp.zeros((256, 128), F32)

    arrived(bx.at[0:256], r_h.at[0])
    arrived(bx.at[768:1024], r_h.at[1])
    arrived(ax.at[0:64], r_h.at[2])
    arrived(ax.at[128:192], r_h.at[3])
    for t in range(3):
        sx[t * 64 : t * 64 + 64] = dot_nt(ax[t * 64 : t * 64 + 64], bx[...]) * (1.0 / 8.0)

    arrived(nb_all.at[0:15], r_nb.at[0])
    nb_own[...] = join(nb_all[...])
    send(nb_own, nb_lo, s_h.at[4], r_h.at[4], up_a)
    send(nb_own, nb_hi, s_h.at[5], r_h.at[5], down_a)
    arrived(na_all.at[0:31], r_na.at[0])
    na_own[...] = join(na_all[...])
    send(na_own, na_lo, s_h.at[6], r_h.at[6], up_b)
    send(na_own, na_hi, s_h.at[7], r_h.at[7], down_b)
    arrived(nb_lo, r_h.at[4])
    arrived(nb_hi, r_h.at[5])
    cols = [
        to_column(jnp.where(me_a > 0, nb_lo[...], FAR)),
        to_column(nb_own[...]),
        to_column(jnp.where(me_a < 31, nb_hi[...], FAR)),
    ]
    arrived(na_lo, r_h.at[6])
    arrived(na_hi, r_h.at[7])
    nar[0:2] = jnp.where(me_b > 0, na_lo[2:4], FAR) - OFFSET
    nar[2:6] = na_own[...] - OFFSET
    nar[6:8] = jnp.where(me_b < 15, na_hi[0:2], FAR) - OFFSET

    for t in range(3):
        for b in range(8):
            v = sx[t * 64 : t * 64 + 64, b * 128 : (b + 1) * 128] - cols[t] - nar[b : b + 1]
            v = jnp.maximum(v, 0.0) + jnp.log(1.0 + jnp.exp(-jnp.abs(v)))
            xt[pl.ds(t * 512 + b, 64, stride=8), :] = v
    lane = iota((48, 128), 1)
    for a2 in range(32):
        rows = [xt[pl.ds(((t * 2 + a) * 32 + a2) * 8, 8), :] for t in range(3) for a in range(2)]
        m = jnp.concatenate(rows, axis=0)
        out = slice((a2 + 1) * 128, (a2 + 2) * 128)
        x3[0:48, out], x3_low[0:48, out] = halves(jnp.where(lane > 0, pltpu.roll(m, 1, 1), 0.0))
        x3[48:96, out], x3_low[48:96, out] = halves(m)
        x3[96:144, out], x3_low[96:144, out] = halves(jnp.where(lane < 127, pltpu.roll(m, 127, 1), 0.0))
    for g in range(8):
        at2 = g * 512
        high, low = (
            jnp.concatenate([x[:, at2 + d * 128 : at2 + d * 128 + 512] for d in range(3)], axis=0)
            for x in (x3, x3_low)
        )
        hidden = dot(w1[...], high)
        hidden = hidden[0:192] + hidden[192:384] + dot(w1[0:192], low)
        high, low = halves(jnp.maximum(hidden + bias, 0.0))
        out = dot(w2[:, 0:192], high)
        zs[:, at2 + 128 : at2 + 640] = out[0:72] + out[72:144] + dot(w2[0:72, 0:192], low)
    lane = iota((8, 128), 1)
    for a2 in range(32):
        u = []
        for d4 in range(3):
            terms = [
                zs[(d * 3 + d4) * 8 : (d * 3 + d4) * 8 + 8, (a2 + d) * 128 : (a2 + d + 1) * 128]
                for d in range(3)
            ]
            u.append(terms[0] + terms[1] + terms[2])
        f = u[1] + jnp.where(lane > 0, pltpu.roll(u[0], 1, 1), 0.0)
        f = f + jnp.where(lane < 127, pltpu.roll(u[2], 127, 1), 0.0)
        ft[a2 * 8 : a2 * 8 + 8] = jnp.maximum(f, 0.0)
    for a in range(2):
        for b in range(4):
            rows, lanes = slice(a * 32, a * 32 + 32), slice(b * 128, (b + 1) * 128)
            rn[rows, lanes] = own[rows, lanes] + ft[pl.ds(a * 4 + b, 32, stride=8), :]

    refined = rn[...]
    lse_c, top_r, sum_r, share = masses(refined)
    for b in range(4):
        na2_src[b : b + 1] = lse_c[:, b * 128 : (b + 1) * 128]
    for dz, dx in AA_STEPS:
        send(na2_src, na2_all.at[me_a], s_na2.at[0], r_na2.at[0], at(dz, dx))
    lse_r = top_r + jnp.log(sum_r)
    nb2_src[:, 0:64] = to_row(lse_r)
    for d in BA_STEPS:
        send(nb2_src, nb2_all.at[me_b], s_nb2.at[0], r_nb2.at[0], (me_a, (me_b + d) & 15))
    na2_all[pl.ds(me_a, 1)] = na2_src[...][None]
    nb2_all[pl.ds(me_b, 1)] = nb2_src[...][None]
    high, low = halves(share)
    features = bx[256:768]
    moved = (dot(high, features) + dot(low, features)) / sum_r
    pn[0:64] = moved[:, 0:128]
    pn[64:128] = moved[:, 128:256]
    pn[128:192] = jnp.broadcast_to(lse_r, (64, 128))
    for g in range(3):
        for q in range(4):
            rows = pl.ds(g * 64 + (q >> 1) * 32 + (q & 1), 16, stride=2)
            ps[pl.ds(g * 4 + q, 16, stride=16), :] = pn[rows, :]
    for d in BA_STEPS:
        to = (me_b + d) & 15
        block = ps.at[pl.ds(pl.multiple_of(to * 16, 16), 16)]
        send(block, pr.at[me_b], s_p.at[0], r_p.at[0], (me_a, to))
    pr[pl.ds(me_b, 1)] = ps[pl.ds(pl.multiple_of(me_b * 16, 16), 16), :][None]

    arrived(nb2_all.at[0:15], r_nb2.at[0])
    col = to_column(join(nb2_all[...])) - OFFSET
    arrived(pr.at[0:15], r_p.at[0])
    lse = pr[:, 8:12, :]
    weight = jnp.exp(lse - jnp.max(lse, axis=0, keepdims=True))
    total = jnp.sum(weight, axis=0)
    for g in range(2):
        moved = jnp.sum(weight * pr[:, g * 4 : g * 4 + 4, :], axis=0) / total
        for a in range(2):
            warped[a, :, g * 128 : g * 128 + 128] = moved[a * 2 : a * 2 + 2]
    twice = 2.0 * refined - col
    arrived(na2_all.at[0:31], r_na2.at[0])
    norm = join(na2_all[...])
    for b in range(4):
        lm[pl.ds(b, 64, stride=4), :] = twice[:, b * 128 : (b + 1) * 128] - norm[b : b + 1]
    for ref, sem in [
        (gb.at[0:31], s_b.at[0]), (ga.at[0:15], s_a.at[0]), (na_all.at[0:31], s_na.at[0]), (nb_all.at[0:15], s_nb.at[0]),
        (na2_all.at[0:31], s_na2.at[0]), (nb2_all.at[0:15], s_nb2.at[0]), (pr.at[0:15], s_p.at[0]),
        (bx.at[0:256], s_h.at[0]), (bx.at[0:256], s_h.at[1]), (ax.at[0:64], s_h.at[2]), (ax.at[0:64], s_h.at[3]),
        (nb_own, s_h.at[4]), (nb_own, s_h.at[5]), (na_own, s_h.at[6]), (na_own, s_h.at[7]),
    ]:
        arrived(ref, sem)


def place_results(lm, warped, lm_out, warped_out, s):
    copies = [pltpu.make_async_copy(lm, lm_out, s.at[0]), pltpu.make_async_copy(warped, warped_out, s.at[1])]
    for copy in copies:
        copy.start()
    for copy in copies:
        copy.wait()


def local(features_a, features_b, conv_in, bias_in, conv_out):
    ci = conv_in.transpose(1, 2, 3, 4, 0).reshape(27, 3, 8)
    co = conv_out.transpose(1, 2, 3, 4, 0).reshape(27, 3, 8)
    dma = pltpu.SemaphoreType.DMA
    vmem = pltpu.VMEM
    lm, warped = pl.pallas_call(
        kernel,
        out_shape=(jax.ShapeDtypeStruct((256, 128), F32), jax.ShapeDtypeStruct((2, 2, 256), F32)),
        in_specs=[pl.BlockSpec(memory_space=pltpu.HBM)] * 5,
        out_specs=(pl.BlockSpec(memory_space=pltpu.VMEM),) * 2,
        scratch_shapes=[
            vmem((2, 2, 256), BF16), vmem((4, 4, 256), BF16), vmem((27, 3, 8), F32), vmem((27, 3, 8), F32), vmem((1, 8), F32),
            vmem((32, 256), F32), vmem((512, 128), F32), vmem((16, 256), BF16), vmem((16, 256), BF16),
            vmem((16, 16, 256), BF16), vmem((32, 16, 256), BF16),
            vmem((192, 256), BF16), vmem((1024, 256), BF16), vmem((512, 512), BF16),
            vmem((192, 512), F32), vmem((384, 432), BF16), vmem((128, 256), F32), vmem((144, 256), BF16),
            vmem((4, 128), F32), vmem((1, 128), F32), vmem((32, 4, 128), F32), vmem((16, 1, 128), F32),
            vmem((4, 128), F32), vmem((1, 128), F32), vmem((4, 128), F32), vmem((4, 128), F32),
            vmem((1, 128), F32), vmem((1, 128), F32),
            vmem((64, 512), F32), vmem((192, 1024), F32), vmem((1536, 128), F32),
            vmem((144, 34 * 128), BF16), vmem((144, 34 * 128), BF16), vmem((72, 34 * 128), F32), vmem((256, 128), F32),
            vmem((64, 512), F32), vmem((192, 128), F32), vmem((256, 128), F32), vmem((16, 16, 128), F32),
            vmem((4, 128), F32), vmem((1, 128), F32), vmem((32, 4, 128), F32), vmem((16, 1, 128), F32),
            vmem((8, 128), F32),
            dma((1,)), dma((1,)), dma((1,)), dma((9,)), dma((8,)), dma((8,)),
            dma((1,)), dma((1,)), dma((1,)), dma((1,)),
            dma((1,)), dma((1,)), dma((1,)), dma((1,)), dma((1,)), dma((1,)), dma((5,)),
        ],
        compiler_params=pltpu.CompilerParams(
            collective_id=0, has_side_effects=True, vmem_limit_bytes=60 * 2**20
        ),
        cost_estimate=pl.CostEstimate(flops=2 * 10**9, bytes_accessed=10**6, transcendentals=10**6),
    )(features_a, features_b, ci, co, bias_in.reshape(1, 8))
    lm = lm.reshape(2, 32, 4, 128)
    return pl.pallas_call(
        place_results,
        out_shape=(jax.ShapeDtypeStruct(lm.shape, F32), jax.ShapeDtypeStruct(warped.shape, F32)),
        in_specs=[pl.BlockSpec(memory_space=pltpu.VMEM)] * 2,
        out_specs=(pl.BlockSpec(memory_space=pltpu.HBM),) * 2,
        scratch_shapes=[dma((2,))],
        compiler_params=pltpu.CompilerParams(vmem_limit_bytes=60 * 2**20),
    )(lm, warped)


def solution(mesh):
    placed = (P("aa", "ba", None), P("ba", "aa", None), P(), P(), P())
    return jax.shard_map(
        local,
        mesh=mesh,
        in_specs=placed,
        out_specs=(P("aa", None, "ba", None), P("aa", "ba", None)),
        check_vma=False,
    )
```

time: 59.6 us -> 53.2 us (0.89)
  local copies, waits for them, and re-layouts: 3.67 us -> 0 us
  Pallas kernels: 55.1 us -> 52.4 us
    pallas_call x1, Pallas kernels: 55.1 us -> 50.8 us  [local(): pl.pallas_call(kernel, out_shape=(jax.ShapeDtypeStruct((256, 128), F32),...]
    reshape x7 -> x0, local copies, waits for them, and re-layouts: 2.31 us -> none  [the longest x2 0.9 us: local(): conv_in.reshape(8, 81)]
    pallas_call x0 -> x1, Pallas kernels: none -> 1.58 us  [local(): pl.pallas_call(place_results, out_shape=(jax.ShapeDtypeStruct(lm.shape, F...]
    unnamed x7 -> x0, local copies, waits for them, and re-layouts: 1.28 us -> none
where the time goes in v2:
time: 53.2 us; the launch traced here: 53 us
  Pallas kernels  52.4 us (98%)
  between operations  0.64 us (1%)
    pallas_call x1, Pallas kernels, local(): pl.pallas_call(kernel, out_shape=(jax.ShapeDtypeStruct((256, 128), F32),...  50.8 us
    pallas_call x1, Pallas kernels, local(): pl.pallas_call(place_results, out_shape=(jax.ShapeDtypeStruct(lm.shape, F...  1.58 us

profile of v2, /device:TPU:1, one launch (start us, length us, event | category | flops | bytes accessed | tf_op | source)
XLA Modules:
  0.0 53.0 jit_solution(6951667035044271976)
XLA Ops:
  0.6 50.8 %shard_map.68 = (f32[256,128]{1,0:T(8,128)}, f32[2,2,256]{2,1,0:T(2,128)}) custom-call(bf16[2,2,256]{2,1,0:T(2,128)(2,1)} %fa_hbm.1, bf16[4,4,256]{2,1,0:T(4,128)(2,1)} %fb_hbm.1, f32[27,3,8]{2,1,0:T(4,128)} %bitcast.9, f32[27,3,8]{2,1,0:T(4,128)} %bitcast.10, f32[1,8]{1,0:T(1,128)} %bitcast.11), custom_call_target="tpu_custom_call" | custom-call | flops 2000000000 | bytes 1000000 | tf_op jit(solution)/shard_map/pallas_call | solution.py:368
  51.4 1.6 %shard_map.69 = (f32[2,32,4,128]{3,2,1,0:T(4,128)}, f32[2,2,256]{2,1,0:T(2,128)}) custom-call(f32[2,32,4,128]{3,2,1,0:T(4,128)} %bitcast.8, f32[2,2,256]{2,1,0:T(2,128)} %get-tuple-element.5.warped), custom_call_target="tpu_custom_call" | custom-call | tf_op jit(solution)/shard_map/pallas_call | solution.py:397

commit v3 on v2

--- a/solution.py
+++ b/solution.py
@@ -75,9 +75,9 @@
 
 def kernel(
     fa_hbm, fb_hbm, ci_hbm, co_hbm, bias_hbm, lm, warped,
-    fa, fb, ci, co, bias_row, stage, taps_m, pa, pb, ga, gb, ax, bx, perm_b, w1f, w1, w2f, w2,
+    fa, fb, ci, co, bias_row, stage, taps_m, pa, pb, ga, gb, ax, bx, w1f, w1, w2f, w2,
     na_src, nb_src, na_all, nb_all, na_own, nb_own, na_lo, na_hi, nb_lo, nb_hi,
-    own, sx, xt, x3, x3_low, zs, ft, rn, pn, ps, pr,
+    own, sx, xt, x3, x3_low, acc, zs, ft, rn, pn, ps, pr,
     na2_src, nb2_src, na2_all, nb2_all, nar,
     s_a, r_a, s_b, r_b, s_h, r_h, s_na, r_na, s_nb, r_nb, s_na2, r_na2, s_nb2, r_nb2, s_p, r_p, s_in,
 ):
@@ -122,8 +122,6 @@
     for b in range(4):
         stage[16 + b * 4 : 20 + b * 4] = fb[b].astype(F32)
     pb[...] = stage[16:32].astype(BF16)
-    ga[pl.ds(me_b, 1)] = pa[...][None]
-    gb[pl.ds(me_a, 1)] = pb[...][None]
     pl.semaphore_wait(barrier, len(greet))
     for k, d in enumerate(NEAR):
         send(pb, gb.at[me_a], s_b.at[0], r_b.at[k], at(d))
@@ -131,10 +129,11 @@
     for d in BA_STEPS:
         send(pa, ga.at[me_b], s_a.at[0], r_a.at[0], (me_a, (me_b + d) & 15))
 
-    row = iota((512, 128), 0)
-    src = ((row >> 2) & 31) * 16 + (row >> 7) * 4 + (row & 3)
-    for g in range(4):
-        perm_b[:, g * 128 : (g + 1) * 128] = one_hot(src == iota((512, 128), 1) + g * 128)
+    ga[pl.ds(me_b, 1)] = pa[...][None]
+    gb[pl.ds(me_a, 1)] = pb[...][None]
+
+    row = iota((128, 128), 0)
+    perm_b = one_hot(((row >> 2) & 7) * 16 + (row >> 5) * 4 + (row & 3) == iota((128, 128), 1))
     row = iota((64, 256), 0)
     perm_a = one_hot(((row & 31) >> 1) * 16 + (row >> 5) * 2 + (row & 1) == iota((64, 256), 1))
 
@@ -154,7 +153,10 @@
     send(ax.at[64:128], ax.at[0:64], s_h.at[2], r_h.at[2], up_a)
     send(ax.at[64:128], ax.at[128:192], s_h.at[3], r_h.at[3], down_a)
     arrived(gb.at[0:23], r_b.at[8])
-    bx[256:768] = dot(perm_b[...], gb[...].reshape(512, 256)).astype(BF16)
+    for g in range(4):
+        rows = dot(perm_b, gb[g * 8 : g * 8 + 8].reshape(128, 256)).astype(BF16)
+        for b in range(4):
+            bx[256 + b * 128 + g * 32 : 288 + b * 128 + g * 32] = rows[b * 32 : b * 32 + 32]
 
     send(bx.at[512:768], bx.at[0:256], s_h.at[0], r_h.at[0], up_b)
     send(bx.at[256:512], bx.at[768:1024], s_h.at[1], r_h.at[1], down_b)
@@ -194,7 +196,17 @@
     for p in range(24):
         s = (p // 6) * 8 + p % 6
         w1f[p * 8 : p * 8 + 8] = pltpu.roll(base, s, 1) if s else base
-    w1[0:192], w1[192:384] = halves(w1f[:, 0:432])
+    for g in range(4):
+        c = iota((8, 128), 1) + (g & 1) * 128
+        d2 = (c * 820) >> 16
+        c = c - 80 * d2
+        d4 = (c * 2731) >> 16
+        c = jnp.where((d4 < 3) & (d2 < 3), c - 24 * d4, -1000)
+        b1 = (c & 3) + (2 if g < 2 else ((c & 2) << 1))
+        target = (d2 * 3 + d4) * 48 + (c >> 2) * 8 + b1
+        chosen = one_hot(iota((512, 128), 0) == jnp.broadcast_to(target[0:1], (512, 128)))
+        for part, rows in zip(halves(w1f[...]), (slice(0, 192), slice(192, 384))):
+            w1[rows, g * 128 : g * 128 + 128] = dot(part, chosen).astype(BF16)
 
     k, c = iota((256, 256), 0) >> 3, iota((256, 256), 1)
     k3 = (k * 11) >> 5
@@ -224,8 +236,8 @@
     bias = jnp.broadcast_to(jnp.sum(bias, axis=1, keepdims=True), (8, 128))
     bias = jnp.concatenate([jnp.concatenate([bias] * 24, axis=0)] * 4, axis=1)
     for x in (x3, x3_low):
-        x[:, 0:128] = jnp.zeros((144, 128), BF16)
-        x[:, 33 * 128 :] = jnp.zeros((144, 128), BF16)
+        x[:, 0:128] = jnp.zeros((160, 128), BF16)
+        x[:, 33 * 128 :] = jnp.zeros((160, 128), BF16)
     zs[:, 0:128] = jnp.zeros((72, 128), F32)
     zs[:, 33 * 128 :] = jnp.zeros((72, 128), F32)
     nb2_src[...] = jnp.zeros((1, 128), F32)
@@ -253,34 +265,45 @@
         to_column(nb_own[...]),
         to_column(jnp.where(me_a < 31, nb_hi[...], FAR)),
     ]
+    nar[2:6] = na_own[...] - OFFSET
+    lane = iota((24, 128), 1)
+
+    def match(side, columns):
+        for t in range(3):
+            for k, b in enumerate(columns):
+                v = sx[t * 64 : t * 64 + 64, b * 128 : (b + 1) * 128] - cols[t] - nar[b : b + 1]
+                v = jnp.maximum(v, 0.0) + jnp.log(1.0 + jnp.exp(-jnp.abs(v)))
+                for a in range(2):
+                    xt[pl.ds(side * 768 + t * 256 + a * 4 + k, 32, stride=8), :] = v[a * 32 : a * 32 + 32]
+        for a2 in range(32):
+            m = jnp.concatenate([xt[pl.ds(side * 768 + (t * 32 + a2) * 8, 8), :] for t in range(3)], axis=0)
+            left = jnp.where(lane > 0, pltpu.roll(m, 1, 1), 0.0)
+            right = jnp.where(lane < 127, pltpu.roll(m, 127, 1), 0.0)
+            m = jnp.concatenate([left, m, right, jnp.zeros((8, 128), F32)], axis=0)
+            rows, out = slice(side * 80, side * 80 + 80), slice((a2 + 1) * 128, (a2 + 2) * 128)
+            x3[rows, out], x3_low[rows, out] = halves(m)
+
+    def first(side, at2):
+        rows, taps = slice(side * 80, side * 80 + 80), slice(side * 256, side * 256 + 240)
+        high, low = (
+            jnp.concatenate([x[rows, at2 + d * 128 : at2 + d * 128 + 512] for d in range(3)], axis=0)
+            for x in (x3, x3_low)
+        )
+        out = dot(w1[:, taps], high)
+        return out[0:192] + out[192:384] + dot(w1[0:192, taps], low)
+
+    match(0, (2, 3, 4, 5))
+    for g in range(8):
+        acc[:, g * 512 : g * 512 + 512] = first(0, g * 512) + bias
     arrived(na_lo, r_h.at[6])
     arrived(na_hi, r_h.at[7])
     nar[0:2] = jnp.where(me_b > 0, na_lo[2:4], FAR) - OFFSET
-    nar[2:6] = na_own[...] - OFFSET
     nar[6:8] = jnp.where(me_b < 15, na_hi[0:2], FAR) - OFFSET
-
-    for t in range(3):
-        for b in range(8):
-            v = sx[t * 64 : t * 64 + 64, b * 128 : (b + 1) * 128] - cols[t] - nar[b : b + 1]
-            v = jnp.maximum(v, 0.0) + jnp.log(1.0 + jnp.exp(-jnp.abs(v)))
-            xt[pl.ds(t * 512 + b, 64, stride=8), :] = v
-    lane = iota((48, 128), 1)
-    for a2 in range(32):
-        rows = [xt[pl.ds(((t * 2 + a) * 32 + a2) * 8, 8), :] for t in range(3) for a in range(2)]
-        m = jnp.concatenate(rows, axis=0)
-        out = slice((a2 + 1) * 128, (a2 + 2) * 128)
-        x3[0:48, out], x3_low[0:48, out] = halves(jnp.where(lane > 0, pltpu.roll(m, 1, 1), 0.0))
-        x3[48:96, out], x3_low[48:96, out] = halves(m)
-        x3[96:144, out], x3_low[96:144, out] = halves(jnp.where(lane < 127, pltpu.roll(m, 127, 1), 0.0))
+    match(1, (0, 1, 6, 7))
     for g in range(8):
         at2 = g * 512
-        high, low = (
-            jnp.concatenate([x[:, at2 + d * 128 : at2 + d * 128 + 512] for d in range(3)], axis=0)
-            for x in (x3, x3_low)
-        )
-        hidden = dot(w1[...], high)
-        hidden = hidden[0:192] + hidden[192:384] + dot(w1[0:192], low)
-        high, low = halves(jnp.maximum(hidden + bias, 0.0))
+        hidden = acc[:, at2 : at2 + 512] + first(1, at2)
+        high, low = halves(jnp.maximum(hidden, 0.0))
         out = dot(w2[:, 0:192], high)
         zs[:, at2 + 128 : at2 + 640] = out[0:72] + out[72:144] + dot(w2[0:72, 0:192], low)
     lane = iota((8, 128), 1)
@@ -374,13 +397,13 @@
             vmem((2, 2, 256), BF16), vmem((4, 4, 256), BF16), vmem((27, 3, 8), F32), vmem((27, 3, 8), F32), vmem((1, 8), F32),
             vmem((32, 256), F32), vmem((512, 128), F32), vmem((16, 256), BF16), vmem((16, 256), BF16),
             vmem((16, 16, 256), BF16), vmem((32, 16, 256), BF16),
-            vmem((192, 256), BF16), vmem((1024, 256), BF16), vmem((512, 512), BF16),
-            vmem((192, 512), F32), vmem((384, 432), BF16), vmem((128, 256), F32), vmem((144, 256), BF16),
+            vmem((192, 256), BF16), vmem((1024, 256), BF16),
+            vmem((192, 512), F32), vmem((384, 512), BF16), vmem((128, 256), F32), vmem((144, 256), BF16),
             vmem((4, 128), F32), vmem((1, 128), F32), vmem((32, 4, 128), F32), vmem((16, 1, 128), F32),
             vmem((4, 128), F32), vmem((1, 128), F32), vmem((4, 128), F32), vmem((4, 128), F32),
             vmem((1, 128), F32), vmem((1, 128), F32),
             vmem((64, 512), F32), vmem((192, 1024), F32), vmem((1536, 128), F32),
-            vmem((144, 34 * 128), BF16), vmem((144, 34 * 128), BF16), vmem((72, 34 * 128), F32), vmem((256, 128), F32),
+            vmem((160, 34 * 128), BF16), vmem((160, 34 * 128), BF16), vmem((192, 4096), F32), vmem((72, 34 * 128), F32), vmem((256, 128), F32),
             vmem((64, 512), F32), vmem((192, 128), F32), vmem((256, 128), F32), vmem((16, 16, 128), F32),
             vmem((4, 128), F32), vmem((1, 128), F32), vmem((32, 4, 128), F32), vmem((16, 1, 128), F32),
             vmem((8, 128), F32),

time: 53.2 us -> 51.6 us (0.970)
  Pallas kernels: 52.4 us -> 50.7 us
    pallas_call x1, Pallas kernels: 50.8 us -> 49.1 us  [local(): pl.pallas_call(kernel, out_shape=(jax.ShapeDtypeStruct((256, 128), F32),...]
where the time goes in v3:
time: 51.6 us; the launch traced here: 51.3 us
  Pallas kernels  50.7 us (98%)
  between operations  0.64 us (1%)
    pallas_call x1, Pallas kernels, local(): pl.pallas_call(kernel, out_shape=(jax.ShapeDtypeStruct((256, 128), F32),...  49.1 us
    pallas_call x1, Pallas kernels, local(): pl.pallas_call(place_results, out_shape=(jax.ShapeDtypeStruct(lm.shape, F...  1.58 us

profile of v3, /device:TPU:1, one launch (start us, length us, event | category | flops | bytes accessed | tf_op | source)
XLA Modules:
  0.0 51.3 jit_solution(12256520467068472818)
XLA Ops:
  0.6 49.1 %shard_map.68 = (f32[256,128]{1,0:T(8,128)}, f32[2,2,256]{2,1,0:T(2,128)}) custom-call(bf16[2,2,256]{2,1,0:T(2,128)(2,1)} %fa_hbm.1, bf16[4,4,256]{2,1,0:T(4,128)(2,1)} %fb_hbm.1, f32[27,3,8]{2,1,0:T(4,128)} %bitcast.9, f32[27,3,8]{2,1,0:T(4,128)} %bitcast.10, f32[1,8]{1,0:T(1,128)} %bitcast.11), custom_call_target="tpu_custom_call" | custom-call | flops 2000000000 | bytes 1000000 | tf_op jit(solution)/shard_map/pallas_call | solution.py:391
  49.7 1.6 %shard_map.69 = (f32[2,32,4,128]{3,2,1,0:T(4,128)}, f32[2,2,256]{2,1,0:T(2,128)}) custom-call(f32[2,32,4,128]{3,2,1,0:T(4,128)} %bitcast.8, f32[2,2,256]{2,1,0:T(2,128)} %get-tuple-element.5.warped), custom_call_target="tpu_custom_call" | custom-call | tf_op jit(solution)/shard_map/pallas_call | solution.py:420

commit v4 on v3

--- a/solution.py
+++ b/solution.py
@@ -11,6 +11,7 @@
 MESH = pl.DeviceIdType.MESH
 OFFSET = math.log(64 * 32 * 64 * 128)
 FAR = 1e30
+WIDE = 2048
 
 AA_STEPS = sorted(
     [(dz, dx) for dz in range(-7, 9) for dx in range(2) if dz or dx],
@@ -234,7 +235,7 @@
     w2[0:72], w2[72:144] = halves(jnp.where(inside, select(order, w2f[...]), 0.0))
     bias = jnp.where(iota((8, 8), 0) == iota((8, 8), 1), bias_row[...], 0.0)
     bias = jnp.broadcast_to(jnp.sum(bias, axis=1, keepdims=True), (8, 128))
-    bias = jnp.concatenate([jnp.concatenate([bias] * 24, axis=0)] * 4, axis=1)
+    bias = jnp.concatenate([jnp.concatenate([bias] * 24, axis=0)] * (WIDE // 128), axis=1)
     for x in (x3, x3_low):
         x[:, 0:128] = jnp.zeros((160, 128), BF16)
         x[:, 33 * 128 :] = jnp.zeros((160, 128), BF16)
@@ -286,28 +287,23 @@
     def first(side, at2):
         rows, taps = slice(side * 80, side * 80 + 80), slice(side * 256, side * 256 + 240)
         high, low = (
-            jnp.concatenate([x[rows, at2 + d * 128 : at2 + d * 128 + 512] for d in range(3)], axis=0)
+            jnp.concatenate([x[rows, at2 + d * 128 : at2 + d * 128 + WIDE] for d in range(3)], axis=0)
             for x in (x3, x3_low)
         )
         out = dot(w1[:, taps], high)
         return out[0:192] + out[192:384] + dot(w1[0:192, taps], low)
 
     match(0, (2, 3, 4, 5))
-    for g in range(8):
-        acc[:, g * 512 : g * 512 + 512] = first(0, g * 512) + bias
+    for g in range(4096 // WIDE):
+        acc[:, g * WIDE : g * WIDE + WIDE] = first(0, g * WIDE) + bias
     arrived(na_lo, r_h.at[6])
     arrived(na_hi, r_h.at[7])
     nar[0:2] = jnp.where(me_b > 0, na_lo[2:4], FAR) - OFFSET
     nar[6:8] = jnp.where(me_b < 15, na_hi[0:2], FAR) - OFFSET
     match(1, (0, 1, 6, 7))
-    for g in range(8):
-        at2 = g * 512
-        hidden = acc[:, at2 : at2 + 512] + first(1, at2)
-        high, low = halves(jnp.maximum(hidden, 0.0))
-        out = dot(w2[:, 0:192], high)
-        zs[:, at2 + 128 : at2 + 640] = out[0:72] + out[72:144] + dot(w2[0:72, 0:192], low)
-    lane = iota((8, 128), 1)
-    for a2 in range(32):
+    side = iota((8, 128), 1)
+
+    def second(a2):
         u = []
         for d4 in range(3):
             terms = [
@@ -315,9 +311,19 @@
                 for d in range(3)
             ]
             u.append(terms[0] + terms[1] + terms[2])
-        f = u[1] + jnp.where(lane > 0, pltpu.roll(u[0], 1, 1), 0.0)
-        f = f + jnp.where(lane < 127, pltpu.roll(u[2], 127, 1), 0.0)
+        f = u[1] + jnp.where(side > 0, pltpu.roll(u[0], 1, 1), 0.0)
+        f = f + jnp.where(side < 127, pltpu.roll(u[2], 127, 1), 0.0)
         ft[a2 * 8 : a2 * 8 + 8] = jnp.maximum(f, 0.0)
+
+    for g in range(4096 // WIDE):
+        at2 = g * WIDE
+        hidden = acc[:, at2 : at2 + WIDE] + first(1, at2)
+        high, low = halves(jnp.maximum(hidden, 0.0))
+        out = dot(w2[:, 0:192], high)
+        zs[:, at2 + 128 : at2 + 128 + WIDE] = out[0:72] + out[72:144] + dot(w2[0:72, 0:192], low)
+        for a2 in range(max(at2 // 128 - 1, 0), (at2 + WIDE) // 128 - 1):
+            second(a2)
+    second(31)
     for a in range(2):
         for b in range(4):
             rows, lanes = slice(a * 32, a * 32 + 32), slice(b * 128, (b + 1) * 128)
@@ -362,10 +368,6 @@
         for a in range(2):
             warped[a, :, g * 128 : g * 128 + 128] = moved[a * 2 : a * 2 + 2]
     twice = 2.0 * refined - col
-    arrived(na2_all.at[0:31], r_na2.at[0])
-    norm = join(na2_all[...])
-    for b in range(4):
-        lm[pl.ds(b, 64, stride=4), :] = twice[:, b * 128 : (b + 1) * 128] - norm[b : b + 1]
     for ref, sem in [
         (gb.at[0:31], s_b.at[0]), (ga.at[0:15], s_a.at[0]), (na_all.at[0:31], s_na.at[0]), (nb_all.at[0:15], s_nb.at[0]),
         (na2_all.at[0:31], s_na2.at[0]), (nb2_all.at[0:15], s_nb2.at[0]), (pr.at[0:15], s_p.at[0]),
@@ -373,6 +375,10 @@
         (nb_own, s_h.at[4]), (nb_own, s_h.at[5]), (na_own, s_h.at[6]), (na_own, s_h.at[7]),
     ]:
         arrived(ref, sem)
+    arrived(na2_all.at[0:31], r_na2.at[0])
+    norm = join(na2_all[...])
+    for b in range(4):
+        lm[pl.ds(b, 64, stride=4), :] = twice[:, b * 128 : (b + 1) * 128] - norm[b : b + 1]
 
 
 def place_results(lm, warped, lm_out, warped_out, s):

time: 51.6 us -> 50.9 us (0.986)
  Pallas kernels: 50.7 us -> 49.9 us
    pallas_call x1, Pallas kernels: 49.1 us -> 48.3 us  [local(): pl.pallas_call(kernel, out_shape=(jax.ShapeDtypeStruct((256, 128), F32),...]
where the time goes in v4:
time: 50.9 us; the launch traced here: 50.5 us
  Pallas kernels  49.9 us (98%)
  between operations  0.64 us (1%)
    pallas_call x1, Pallas kernels, local(): pl.pallas_call(kernel, out_shape=(jax.ShapeDtypeStruct((256, 128), F32),...  48.3 us
    pallas_call x1, Pallas kernels, local(): pl.pallas_call(place_results, out_shape=(jax.ShapeDtypeStruct(lm.shape, F...  1.58 us

profile of v4, /device:TPU:1, one launch (start us, length us, event | category | flops | bytes accessed | tf_op | source)
XLA Modules:
  0.0 50.5 jit_solution(17271191539437547935)
XLA Ops:
  0.6 48.3 %shard_map.68 = (f32[256,128]{1,0:T(8,128)}, f32[2,2,256]{2,1,0:T(2,128)}) custom-call(bf16[2,2,256]{2,1,0:T(2,128)(2,1)} %fa_hbm.1, bf16[4,4,256]{2,1,0:T(4,128)(2,1)} %fb_hbm.1, f32[27,3,8]{2,1,0:T(4,128)} %bitcast.9, f32[27,3,8]{2,1,0:T(4,128)} %bitcast.10, f32[1,8]{1,0:T(1,128)} %bitcast.11), custom_call_target="tpu_custom_call" | custom-call | flops 2000000000 | bytes 1000000 | tf_op jit(solution)/shard_map/pallas_call | solution.py:397
  48.9 1.6 %shard_map.69 = (f32[2,32,4,128]{3,2,1,0:T(4,128)}, f32[2,2,256]{2,1,0:T(2,128)}) custom-call(f32[2,32,4,128]{3,2,1,0:T(4,128)} %bitcast.8, f32[2,2,256]{2,1,0:T(2,128)} %get-tuple-element.5.warped), custom_call_target="tpu_custom_call" | custom-call | tf_op jit(solution)/shard_map/pallas_call | solution.py:426

commit v5 on v4

--- a/solution.py
+++ b/solution.py
@@ -290,8 +290,9 @@
             jnp.concatenate([x[rows, at2 + d * 128 : at2 + d * 128 + WIDE] for d in range(3)], axis=0)
             for x in (x3, x3_low)
         )
-        out = dot(w1[:, taps], high)
-        return out[0:192] + out[192:384] + dot(w1[0:192, taps], low)
+        tall = jnp.concatenate([high, high, low], axis=0)
+        wide = jnp.concatenate([w1[0:192, taps], w1[192:384, taps], w1[0:192, taps]], axis=1)
+        return dot(wide, tall)
 
     match(0, (2, 3, 4, 5))
     for g in range(4096 // WIDE):

time: 50.9 us -> 50.7 us (level)
  no operation moved by 1% of the time
where the time goes in v5:
time: 50.7 us; the launch traced here: 50.4 us
  Pallas kernels  49.8 us (98%)
  between operations  0.64 us (1%)
    pallas_call x1, Pallas kernels, local(): pl.pallas_call(kernel, out_shape=(jax.ShapeDtypeStruct((256, 128), F32),...  48.2 us
    pallas_call x1, Pallas kernels, local(): pl.pallas_call(place_results, out_shape=(jax.ShapeDtypeStruct(lm.shape, F...  1.58 us

profile of v5, /device:TPU:1, one launch (start us, length us, event | category | flops | bytes accessed | tf_op | source)
XLA Modules:
  0.0 50.4 jit_solution(15794920581885563443)
XLA Ops:
  0.6 48.2 %shard_map.68 = (f32[256,128]{1,0:T(8,128)}, f32[2,2,256]{2,1,0:T(2,128)}) custom-call(bf16[2,2,256]{2,1,0:T(2,128)(2,1)} %fa_hbm.1, bf16[4,4,256]{2,1,0:T(4,128)(2,1)} %fb_hbm.1, f32[27,3,8]{2,1,0:T(4,128)} %bitcast.9, f32[27,3,8]{2,1,0:T(4,128)} %bitcast.10, f32[1,8]{1,0:T(1,128)} %bitcast.11), custom_call_target="tpu_custom_call" | custom-call | flops 2000000000 | bytes 1000000 | tf_op jit(solution)/shard_map/pallas_call | solution.py:398
  48.8 1.6 %shard_map.69 = (f32[2,32,4,128]{3,2,1,0:T(4,128)}, f32[2,2,256]{2,1,0:T(2,128)}) custom-call(f32[2,32,4,128]{3,2,1,0:T(4,128)} %bitcast.8, f32[2,2,256]{2,1,0:T(2,128)} %get-tuple-element.5.warped), custom_call_target="tpu_custom_call" | custom-call | tf_op jit(solution)/shard_map/pallas_call | solution.py:427
